TPU v7x, 32 devices: a whole 2x2x4 slice. The times are simulated.
32 devices in a mesh: groups: 2 (over y), row: 2 (over x), col: 4 (over z), rep: 2 (over core).
Axes of the slice: x: 2, y: 2, z: 4, core: 2. Of those that a mesh axis runs over, the one named last changes fastest.
Arguments:
- left_features: bfloat16 [32, 8192], P(('groups', 'row', 'col'), 'rep'), parts along dimension 0, may hold values from -6 to 6
- right_features: bfloat16 [32, 8192], P(('groups', 'col', 'row'), 'rep'), parts along dimension 0, may hold values from -6 to 6
- weight: bfloat16 [1024, 128], replicated, may hold values from -3 to 3
- bias: float32 [128], replicated, may hold values from -4 to 4
- cotangent: bfloat16 [32, 16, 128], P(('groups', 'row'), 'col'), parts along dimension 0, may hold values from -0.59765625 to 0.59765625
Outputs:
- pair_out: float32 [32, 16, 128], P(('groups', 'row'), ('col', 'rep')), parts along dimension 0
- left_grad: bfloat16 [32, 8192], P(('groups', 'row', 'col'), 'rep'), parts along dimension 0
- right_grad: bfloat16 [32, 8192], P(('groups', 'col', 'row'), 'rep'), parts along dimension 0
- weight_grad: float32 [2048, 128], P('groups'), parts along dimension 0
There are 2 independent parts, one for each index of `groups`. A program takes and returns all parts, laid end to end along the dimension named above; an argument that names none is the same for every part. Nothing has to cross between parts.
All inputs are finite; a program needn't handle non-finite values.
Results may differ from a plain program's by a relative error of at most 0.0049.
Values may be sent and summed in bfloat16 or wider, within the bound.
No kernel may reach another device: no remote copies, remote signals or barrier semaphores. Data moves between devices by JAX's collectives and lax.ppermute only.
A program may use at most 64 MiB of HBM per device.

v0:
```python
import jax
import jax.numpy as jnp
from jax import lax
from jax.sharding import PartitionSpec as P

C = 32
S = 256


def on_device(left_features, right_features, weight, bias, cotangent):
    left_rows = lax.all_gather(left_features, "col", axis=0, tiled=True)
    right_rows = lax.all_gather(right_features, "row", axis=0, tiled=True)
    row_count = left_rows.shape[0]
    col_count = right_rows.shape[0]
    out_width = weight.shape[1]
    left_block = left_rows.reshape(row_count, -1, C)
    right_block = right_rows.reshape(col_count, -1, C)
    outer_sum = jnp.einsum(
        "isc,jsd->ijcd", left_block, right_block, preferred_element_type=jnp.float32
    )
    half_mean = (outer_sum / S).astype(jnp.bfloat16).reshape(row_count * col_count, C * C)
    proj_part = jnp.dot(half_mean, weight, preferred_element_type=jnp.float32).reshape(
        row_count, col_count, out_width
    )
    pair_sum = lax.psum_scatter(proj_part, "rep", scatter_dimension=1, tiled=True)
    pair_out = pair_sum + bias
    flat_grad = cotangent.reshape(row_count * col_count, out_width)
    weight_part = jnp.einsum("pk,pe->ke", half_mean, flat_grad, preferred_element_type=jnp.float32)
    weight_grad = lax.psum(weight_part, ("row", "col", "rep"))
    grad_mean = jnp.einsum("pe,ke->pk", flat_grad, weight, preferred_element_type=jnp.float32) / S
    grad_mean = grad_mean.astype(jnp.bfloat16).reshape(row_count, col_count, C, C)
    left_part = jnp.einsum(
        "ijcd,jsd->isc", grad_mean, right_block, preferred_element_type=jnp.float32
    ).reshape(row_count, -1)
    right_part = jnp.einsum(
        "ijcd,isc->jsd", grad_mean, left_block, preferred_element_type=jnp.float32
    ).reshape(col_count, -1)
    left_sum = lax.psum_scatter(left_part, "col", scatter_dimension=0, tiled=True)
    right_sum = lax.psum_scatter(right_part, "row", scatter_dimension=0, tiled=True)
    return (pair_out, left_sum.astype(jnp.bfloat16), right_sum.astype(jnp.bfloat16), weight_grad)


def solution(mesh):
    in_specs = (
        P(("groups", "row", "col"), "rep"),
        P(("groups", "col", "row"), "rep"),
        P(),
        P(),
        P(("groups", "row"), "col", None),
    )
    out_specs = (
        P(("groups", "row"), ("col", "rep"), None),
        P(("groups", "row", "col"), "rep"),
        P(("groups", "col", "row"), "rep"),
        P("groups", None),
    )
    return jax.shard_map(
        on_device, mesh=mesh, in_specs=in_specs, out_specs=out_specs, check_vma=False
    )
```

profile of v0, /device:TPU:0, one launch (start us, length us, event | category | flops | bytes accessed | tf_op | source)
XLA Modules:
  0.0 134.6 jit_solution(2331987500989539474)
XLA Ops:
  8.0 0.0 copy-start
  8.0 0.0 reduce-scatter.2.cloned.1.call-start
  8.1 0.0 copy-start.2
  8.1 5.7 %all-gather = bf16[2,2,4096]{2,1,0:T(2,128)(2,1)S(1)} all-gather(bf16[1,2,4096]{2,1,0:T(2,128)(2,1)} %bitcast.50), channel_id=1, replica_groups=mesh['groups'=2,'row'=2,'col'=4,'rep'=2] {'row'}, dimensions={0}, use_global_device_ids=true | all-gather | bytes 49152 | tf_op jit(solution)/shard_map/all_gather | solution.py:12
  13.8 0.0 copy-done.2
  13.8 13.9 %all-gather.1 = bf16[4,2,4096]{2,1,0:T(2,128)(2,1)S(1)} all-gather(bf16[1,2,4096]{2,1,0:T(2,128)(2,1)S(1)} %bitcast.51), channel_id=1, replica_groups=mesh['groups'=2,'row'=2,'col'=4,'rep'=2] {'col'}, dimensions={0}, use_global_device_ids=true | all-gather | bytes 81920 | tf_op jit(solution)/shard_map/all_gather | solution.py:11
  27.7 0.1 reshape.33
  27.8 0.2 reshape.34
  28.0 0.3 fusion.1
  28.3 0.2 copy.23
  28.5 0.3 dot_general.21
  28.7 0.0 copy-done
  28.7 0.8 fusion.4
  29.5 0.0 reduce-scatter.2.cloned.1.call-update
  29.5 0.0 all-reduce.5.cloned.1.call-start
  29.6 0.2 copy.29
  29.8 0.0 copy-start.1
  29.8 0.3 reshape.39
  30.1 0.4 copy-done.1
  30.5 1.1 fusion.9
  31.5 0.0 all-reduce.5.cloned.1.call-update
  31.6 0.2 fusion.2
  31.7 0.2 reshape.36
  31.9 0.2 convolution_bitcast_fusion
  32.2 0.3 convolution_bitcast_fusion.1
  32.4 0.0 copy-start.5
  32.5 0.6 copy-done.5
  33.1 0.0 copy-start.4
  33.1 0.6 dynamic-slice.2
  33.7 0.1 copy-done.4
  33.8 0.6 dynamic-slice
  35.6 0.1 copy.28
  35.8 0.2 reshape.38
  35.9 8.9 %all-reduce.1 = bf16[4,4096]{1,0:T(4,128)(2,1)S(1)} all-reduce(f32[4,4096]{1,0:T(4,128)S(1)} %reshape.38), channel_id=4, replica_groups=mesh['groups'=2,'row'=2,'col'=4,'rep'=2] {'row'}, use_global_device_ids=true, to_apply=%region_2.0.clone | all-reduce | flops 16384 | bytes 98304
  44.9 0.2 copy.25
  45.1 0.2 reshape.37
  45.3 21.8 %all-reduce.6 = bf16[8,4096]{1,0:T(8,128)(2,1)S(1)} all-reduce(f32[8,4096]{1,0:T(8,128)S(1)} %reshape.37), channel_id=3, replica_groups=mesh['groups'=2,'row'=2,'col'=4,'rep'=2] {'col'}, use_global_device_ids=true, to_apply=%region_1.0.clone | all-reduce | flops 32768 | bytes 196608
  67.2 0.6 dynamic-slice_convert_fusion
  67.8 0.0 copy-start.3
  67.8 0.6 dynamic-slice_convert_fusion.1
  68.4 0.0 reduce-scatter.2.cloned.1.call-done
  68.4 0.0 copy-done.3
  68.5 0.7 broadcast_add_fusion
  69.2 0.6 copy.30
  69.8 55.6 %all-reduce.5.cloned.1.call-done = f32[1024,128]{1,0:T(8,128)} async-done(((f32[1024,128]{1,0:T(8,128)}), f32[1024,128]{1,0:T(8,128)}) %all-reduce.5.cloned.1.call-update) | async-done | bytes 524304 | tf_op jit(solution)/shard_map/psum | solution.py:29
  125.3 1.9 %copy.46 = f32[1024,128]{1,0:T(8,128)} copy(f32[1024,128]{1,0:T(8,128)} %all-reduce.5.cloned.1.call-done) | data formatting | bytes 1048576
Async XLA Ops:
  8.0 20.7 %copy-start = (bf16[1024,128]{1,0:T(8,128)(2,1)S(1)}, bf16[1024,128]{1,0:T(8,128)(2,1)}, u32[]{:S(2)}) copy-start(bf16[1024,128]{1,0:T(8,128)(2,1)} %param.7) | copy-start | bytes 786436
  8.0 60.4 %reduce-scatter.2.cloned.1.call-start = ((), (), s32[]{:S(2)}) async-start(), calls=%async_computation.1 | async-start | bytes 24576 | tf_op jit(solution)/shard_map/reduce_scatter | solution.py:25
  8.1 5.7 %copy-start.2 = (bf16[2,4096]{1,0:T(2,128)(2,1)S(1)}, bf16[2,4096]{1,0:T(2,128)(2,1)}, u32[]{:S(2)}) copy-start(bf16[2,4096]{1,0:T(2,128)(2,1)} %param.5) | copy-start | bytes 49156
  29.5 95.8 %all-reduce.5.cloned.1.call-start = ((), (), s32[]{:S(2)}) async-start(), calls=%async_computation.2 | async-start | bytes 1048576 | tf_op jit(solution)/shard_map/psum | solution.py:29
  29.8 0.7 copy-start.1
  32.4 0.7 copy-start.5
  33.1 0.7 copy-start.4
  67.8 0.7 copy-start.3
Sparse Core Ops, SparseCore 0:
  29.7 8.3 reduce-scatter.1
Sparse Core Ops, SparseCore 1:
  34.0 91.3 all-reduce.4
where the time goes:
time: 135 us
  waiting for transfers between devices  55.6 us (41%)
  blocking collectives  50.4 us (37%)
  between operations  16.9 us (13%)
  local copies, waits for them, and re-layouts  8.2 us (6%)
  matrix products  2.74 us (2%)
    psum x1, waiting for transfers between devices, on_device(): weight_grad = lax.psum(weight_part, ('row', 'col', 'rep'))  55.6 us
    unnamed x2, blocking collectives  30.8 us
    all_gather x1, blocking collectives, on_device(): left_rows = lax.all_gather(left_features, 'col', axis=0, tiled=True)  13.9 us
    all_gather x1, blocking collectives, on_device(): right_rows = lax.all_gather(right_features, 'row', axis=0, tiled=True)  5.72 us
    unnamed x16, local copies, waits for them, and re-layouts  4.81 us
  transfers between devices with their start and end apart: 2, of which 1 were waited for; matrix products, arithmetic and copies ran while one was open for 5% of the time, Pallas kernels for 0%

commit v1 on v0

--- a/solution.py
+++ b/solution.py
@@ -1,13 +1,21 @@
+import functools
+
 import jax
 import jax.numpy as jnp
 from jax import lax
+from jax.experimental import pallas as pl
+from jax.experimental.pallas import tpu as pltpu
 from jax.sharding import PartitionSpec as P
 
 C = 32
 S = 256
-
-
-def on_device(left_features, right_features, weight, bias, cotangent):
+LANES = 128
+F32 = jnp.float32
+BF16 = jnp.bfloat16
+NT = (((1,), (1,)), ((), ()))
+
+
+def tile_plan(left_features, right_features, weight, bias, cotangent):
     left_rows = lax.all_gather(left_features, "col", axis=0, tiled=True)
     right_rows = lax.all_gather(right_features, "row", axis=0, tiled=True)
     row_count = left_rows.shape[0]
@@ -40,7 +48,191 @@
     return (pair_out, left_sum.astype(jnp.bfloat16), right_sum.astype(jnp.bfloat16), weight_grad)
 
 
+def exchange(x, axis, flip, size):
+    return lax.ppermute(x, axis, [(k, k ^ flip) for k in range(size)])
+
+
+def sort_kernel(rows, cols, where, near, far, feats, cot, scratch):
+    tokens = 2 * rows * cols
+    span = tokens * C
+    my_row, my_col = where[0], where[1]
+    for half, block in enumerate((near, far)):
+        for slot in range(cols):
+            row = lax.rem(my_row + half, rows)
+            col = my_col ^ slot
+            left_token = (row * cols + col) * 2
+            for t in range(2):
+                scratch[pl.ds(left_token + t, C, stride=tokens), :] = block[slot, t * C:(t + 1) * C, :].astype(F32)
+            right_at = pl.multiple_of(span + (col * rows + row) * 2 * C, 2 * C)
+            feats[pl.ds(right_at, 2 * C), :] = block[slot, 2 * C:4 * C, :]
+            per_row, per_col = tokens // rows, tokens // cols
+            for j in range(per_col):
+                at = pl.multiple_of((col * per_col + j) * tokens + row * per_row, per_row)
+                first = 4 * C + j * per_row
+                cot[pl.ds(at, per_row), :] = block[slot, first:first + per_row, :].astype(F32)
+    feats[:span, :] = scratch[...].astype(BF16)
+
+
+def feature_grad(outer_weight, cot_rows, features, tokens):
+    copies = LANES // tokens
+    repeated = jnp.concatenate([jnp.concatenate([rows] * copies, axis=0) for rows in cot_rows], axis=0).astype(BF16)
+    grads = lax.dot_general(outer_weight, repeated, NT, preferred_element_type=F32)
+    copy_of = lax.broadcasted_iota(jnp.int32, (C, LANES), 1) // tokens
+    out = []
+    for two in range(2):
+        lanes = grads[:, two * LANES:(two + 1) * LANES]
+        parts = []
+        for group in range(C // copies):
+            first = group * copies * C
+            part = lanes[first:first + C, :]
+            for k in range(1, copies):
+                at = first + k * C
+                part = jnp.where(copy_of == k, lanes[at:at + C, :], part)
+            parts.append((part * (1.0 / S)).astype(BF16))
+        out.append(jnp.concatenate(parts, axis=1))
+    return jnp.dot(jnp.concatenate(out, axis=0), features, preferred_element_type=F32)
+
+
+def grads_kernel(rows, cols, where, feats, cot, weight, weight_dc, left_grad, right_grad, scratch):
+    tokens = 2 * rows * cols
+    span = tokens * C
+    my_row, my_col = where[0], where[1]
+    for j in range(tokens):
+        at = span + j * C
+        scratch[pl.ds(j, C, stride=tokens), :] = feats[at:at + C, :].astype(F32)
+    left_token = (my_row * cols + my_col) * 2
+    cot_rows = [cot[pl.ds(left_token + t, tokens, stride=tokens), :] for t in range(2)]
+    left_grad[...] = feature_grad(weight_dc[...], cot_rows, scratch[...].astype(BF16), tokens)
+    right_token = (my_col * rows + my_row) * 2
+    cot_rows = [cot[pl.ds(pl.multiple_of((right_token + t) * tokens, tokens), tokens), :] for t in range(2)]
+    right_grad[...] = feature_grad(weight[...], cot_rows, feats[:span, :], tokens)
+
+
+def swap_blocks(blocks, width):
+    count = len(blocks)
+    lane_block = lax.broadcasted_iota(jnp.int32, blocks[0].shape, 1) // width
+    bit = 1
+    while bit < count:
+        upper = (lane_block & bit) != 0
+        out = list(blocks)
+        for a in range(count):
+            if a & bit == 0:
+                low, high = blocks[a], blocks[a | bit]
+                out[a] = jnp.where(upper, pltpu.roll(high, bit * width, 1), low)
+                out[a | bit] = jnp.where(upper, high, pltpu.roll(low, LANES - bit * width, 1))
+        blocks = out
+        bit *= 2
+    return blocks
+
+
+def outer_kernel(rows, cols, where, own, other, cot, weight_t, bias, pair_out, weight_grad, scratch, pair_scratch):
+    tokens = 2 * rows * cols
+    span = tokens * C
+    my_row, my_col, my_rep = where[0], where[1], where[2]
+    scratch[my_rep] = own[...]
+    scratch[1 - my_rep] = other[...]
+    count = LANES // tokens
+    right = jnp.concatenate([scratch[0, span:, :], scratch[1, span:, :]], axis=1)
+    cot_all = cot[...].astype(BF16)
+    pair_t = jnp.zeros((weight_t.shape[0], tokens * tokens), F32)
+    for g in range(C // count):
+        lanes = slice(g * LANES, (g + 1) * LANES)
+        left = jnp.concatenate([scratch[0, lanes, :], scratch[1, lanes, :]], axis=1)
+        outer = lax.dot_general(right, left, NT, preferred_element_type=F32) * (1.0 / S)
+        parts = []
+        for h in range(tokens // count):
+            first = h * count * C
+            blocks = [outer[first + k * C:first + (k + 1) * C, :] for k in range(count)]
+            parts.append(jnp.concatenate(swap_blocks(blocks, tokens), axis=0).astype(BF16))
+        mean = jnp.concatenate(parts, axis=1)
+        at = slice(g * count * C, (g + 1) * count * C)
+        weight_grad[at, :] = jnp.dot(mean, cot_all, preferred_element_type=F32)
+        pair_t += jnp.dot(weight_t[:, at], mean, preferred_element_type=F32)
+    pair_scratch[...] = pair_t.T
+    per_row, per_col = tokens // rows, tokens // cols
+    for j in range(per_col // 2):
+        col = my_col * per_col + my_rep * (per_col // 2) + j
+        at = pl.multiple_of(col * tokens + my_row * per_row, per_row)
+        pair_out[:, j, :] = pair_scratch[pl.ds(at, per_row), :] + bias[...]
+
+
+def gather_plan(rows, cols, left_features, right_features, weight, bias, cotangent):
+    held, width = left_features.shape
+    seqs = width // C
+    tokens = held * rows * cols
+    span = tokens * C
+    e = weight.shape[1]
+    vmem = pl.BlockSpec(memory_space=pltpu.VMEM)
+    smem = pl.BlockSpec(memory_space=pltpu.SMEM)
+    params = pltpu.CompilerParams(vmem_limit_bytes=32 * 1024 * 1024)
+    where = jnp.stack([lax.axis_index("row"), lax.axis_index("col"), lax.axis_index("rep")]).astype(jnp.int32)
+
+    def turned(x):
+        return x.reshape(held, seqs, C).transpose(0, 2, 1).reshape(held * C, seqs)
+
+    cot_block = cotangent.transpose(1, 0, 2).reshape(-1, e)
+    block = jnp.concatenate([turned(left_features), turned(right_features), cot_block], axis=0)[None]
+    flip = 1
+    while flip < cols:
+        block = jnp.concatenate([block, exchange(block, "col", flip, cols)], axis=0)
+        flip *= 2
+    far = exchange(block, "row", 1, rows)
+
+    feats, cot = pl.pallas_call(
+        functools.partial(sort_kernel, rows, cols),
+        out_shape=(
+            jax.ShapeDtypeStruct((2 * span, seqs), BF16),
+            jax.ShapeDtypeStruct((tokens * tokens, e), F32),
+        ),
+        in_specs=[smem, vmem, vmem],
+        out_specs=(vmem, vmem),
+        scratch_shapes=[pltpu.VMEM((span, seqs), F32)],
+        compiler_params=params,
+        name="sort_tokens",
+    )(where, block, far)
+    other = exchange(feats, "rep", 1, 2)
+
+    weight_dc = weight.reshape(C, C, e).transpose(1, 0, 2).reshape(C * C, e)
+    left_grad, right_grad = pl.pallas_call(
+        functools.partial(grads_kernel, rows, cols),
+        out_shape=(jax.ShapeDtypeStruct((held * C, seqs), F32),) * 2,
+        in_specs=[smem] + [vmem] * 4,
+        out_specs=(vmem, vmem),
+        scratch_shapes=[pltpu.VMEM((span, seqs), F32)],
+        compiler_params=params,
+        name="feature_grads",
+    )(where, feats, cot, weight, weight_dc)
+
+    pair_out, weight_grad = pl.pallas_call(
+        functools.partial(outer_kernel, rows, cols),
+        out_shape=(
+            jax.ShapeDtypeStruct((tokens // rows, tokens // cols // 2, e), F32),
+            jax.ShapeDtypeStruct((C * C, e), F32),
+        ),
+        in_specs=[smem] + [vmem] * 5,
+        out_specs=(vmem, vmem),
+        scratch_shapes=[pltpu.VMEM((2, 2 * span, seqs), BF16), pltpu.VMEM((tokens * tokens, e), F32)],
+        compiler_params=params,
+        name="outer_mean",
+    )(where, feats, other, cot, weight.T, bias.reshape(1, e))
+
+    def turned_back(x):
+        return x.reshape(held, C, seqs).transpose(0, 2, 1).reshape(held, width).astype(BF16)
+
+    return pair_out, turned_back(left_grad), turned_back(right_grad), weight_grad
+
+
 def solution(mesh):
+    rows, cols = mesh.shape["row"], mesh.shape["col"]
+
+    def on_device(left_features, right_features, weight, bias, cotangent):
+        held, width = left_features.shape
+        tokens = held * rows * cols
+        small = held == 2 and rows == 2 and cols & (cols - 1) == 0 and LANES % tokens == 0 and tokens % 16 == 0
+        if small and width == LANES * C and weight.shape[1] == LANES and C % (LANES // tokens) == 0:
+            return gather_plan(rows, cols, left_features, right_features, weight, bias, cotangent)
+        return tile_plan(left_features, right_features, weight, bias, cotangent)
+
     in_specs = (
         P(("groups", "row", "col"), "rep"),
         P(("groups", "col", "row"), "rep"),

time: 135 us -> 27.5 us (0.20)
  the two profiles are of different devices: /device:TPU:0 before, /device:TPU:29 now
where the time goes in v1:
time: 27.5 us; the launch traced here: 27.1 us
  waiting for transfers between devices  10.5 us (38%)
  starting transfers between devices  5.82 us (21%)
  Pallas kernels  5.63 us (20%)
  local copies, waits for them, and re-layouts  4.33 us (16%)
  between operations  0.73 us (3%)
    ppermute x4, waiting for transfers between devices, exchange(): return lax.ppermute(x, axis, [(k, k ^ flip) for k in range(size)])  10.5 us
    ppermute x4, starting transfers between devices, exchange(): return lax.ppermute(x, axis, [(k, k ^ flip) for k in range(size)])  5.82 us
    pallas_call x1, Pallas kernels, gather_plan(): pl.pallas_call(functools.partial(outer_kernel, rows, cols), out_shape=(ja...  3.42 us
    convert_element_type x4, local copies, waits for them, and re-layouts, turned_back(): x.reshape(held, C, seqs).transpose(0, 2, 1).reshape(held, width)  1.71 us
    pallas_call x1, Pallas kernels, gather_plan(): pl.pallas_call(functools.partial(grads_kernel, rows, cols), out_shape=(ja...  1.52 us
    unnamed x9, local copies, waits for them, and re-layouts  1.45 us
    transpose x1, local copies, waits for them, and re-layouts, gather_plan(): cot_block = cotangent.transpose(1, 0, 2).reshape(-1, e)  0.71 us
    pallas_call x1, Pallas kernels, gather_plan(): pl.pallas_call(functools.partial(sort_kernel, rows, cols), out_shape=(jax...  0.69 us
  transfers between devices with their start and end apart: 4, of which 3 were waited for; matrix products, arithmetic and copies ran while one was open for 8% of the time, Pallas kernels for 6%

profile of v1, /device:TPU:29, one launch (start us, length us, event | category | flops | bytes accessed | tf_op | source)
XLA Modules:
  0.0 27.1 jit_solution(4831243675498613857)
XLA Ops:
  0.6 0.0 copy-start.2
  0.6 0.7 %copy.24 = bf16[4,8,128]{2,1,0:T(8,128)(2,1)S(1)} copy(bf16[4,8,128]{2,0,1:T(4,128)(2,1)} %bitcast.36) | data formatting | bytes 16384 | tf_op jit(solution)/shard_map/transpose | solution.py:173
  1.3 0.0 copy-done.2
  1.4 0.1 reshape.42
  1.5 0.0 copy-start.3
  1.5 0.1 copy.17
  1.5 0.6 %copy-done.3 = bf16[2,4096]{1,0:T(2,128)(2,1)S(1)} copy-done((bf16[2,4096]{1,0:T(2,128)(2,1)S(1)}, bf16[2,4096]{1,0:T(2,128)(2,1)}, u32[]{:S(2)}) %copy-start.3) | copy-done | bytes 16408
  2.2 0.1 reshape.40
  2.3 0.1 copy.16
  2.4 0.2 collective-permute-start
  2.6 2.7 %collective-permute-done = bf16[1,160,128]{2,1,0:T(8,128)(2,1)S(1)} collective-permute-done((bf16[1,160,128]{2,1,0:T(8,128)(2,1)S(1)}, bf16[1,160,128]{2,1,0:T(8,128)(2,1)S(1)}, u32[]{:S(2)}, u32[]{:S(2)}) %collective-permute-start) | collective-permute-done | bytes 40992 | tf_op jit(solution)/shard_map/ppermute | solution.py:52
  5.3 0.0 copy-start
  5.3 0.1 collective-permute-start.1
  5.4 4.9 %collective-permute-done.1 = bf16[2,160,128]{2,1,0:T(8,128)(2,1)S(1)} collective-permute-done((bf16[2,160,128]{2,1,0:T(8,128)(2,1)S(1)}, bf16[2,160,128]{2,1,0:T(8,128)(2,1)S(1)}, u32[]{:S(2)}, u32[]{:S(2)}) %collective-permute-start.1) | collective-permute-done | bytes 81952 | tf_op jit(solution)/shard_map/ppermute | solution.py:52
  10.4 1.3 %collective-permute-start.2 = (bf16[4,160,128]{2,1,0:T(8,128)(2,1)S(1)}, bf16[4,160,128]{2,1,0:T(8,128)(2,1)S(1)}, u32[]{:S(2)}, u32[]{:S(2)}) collective-permute-start(bf16[4,160,128]{2,1,0:T(8,128)(2,1)S(1)} %pad_maximum_fusion.near), channel_id=1, source_target_pairs={{0,8},{8,0},{1,9},{9,1},{2,10},{10,2},{3,11},{11,3},{4,12},{12,4},... | collective-permute-start | bytes 491528 | tf_op jit(solution)/shard_map/ppermute | solution.py:52
  11.6 0.1 pad_add_fusion.where
  11.7 2.9 %collective-permute-done.2.far = bf16[4,160,128]{2,1,0:T(8,128)(2,1)S(1)} collective-permute-done((bf16[4,160,128]{2,1,0:T(8,128)(2,1)S(1)}, bf16[4,160,128]{2,1,0:T(8,128)(2,1)S(1)}, u32[]{:S(2)}, u32[]{:S(2)}) %collective-permute-start.2) | collective-permute-done | bytes 163872 | tf_op jit(solution)/shard_map/ppermute | solution.py:52
  14.6 0.7 %sort_tokens.1 = (bf16[1024,128]{1,0:T(8,128)(2,1)S(1)}, f32[256,128]{1,0:T(8,128)S(1)}) custom-call(s32[3]{0:T(128)S(1)} %pad_add_fusion.where, bf16[4,160,128]{2,1,0:T(8,128)(2,1)S(1)} %pad_maximum_fusion.near, bf16[4,160,128]{2,1,0:T(8,128)(2,1)S(1)} %collective-permute-done.2.far), custom_call_target="tpu_custom_call" | custom-call | tf_op jit(solution)/shard_map/sort_tokens/pallas_call | solution.py:181
  15.3 4.2 %collective-permute-start.3 = (bf16[1024,128]{1,0:T(8,128)(2,1)S(1)}, bf16[1024,128]{1,0:T(8,128)(2,1)S(1)}, u32[]{:S(2)}, u32[]{:S(2)}) collective-permute-start(bf16[1024,128]{1,0:T(8,128)(2,1)S(1)} %get-tuple-element.10.own.feats), channel_id=1, source_target_pairs={{0,1},{1,0},{2,3},{3,2},{4,5},{5,4},{6,7},{7,6},{8,9},{9,8},{10,11... | collective-permute-start | bytes 786440 | tf_op jit(solution)/shard_map/ppermute | solution.py:52
  19.5 0.0 copy-done
  19.5 0.1 copy.19
  19.6 0.1 copy.20
  19.8 1.5 %feature_grads.1 = (f32[64,128]{1,0:T(8,128)S(1)}, f32[64,128]{1,0:T(8,128)S(1)}) custom-call(s32[3]{0:T(128)S(1)} %pad_add_fusion.where, bf16[1024,128]{1,0:T(8,128)(2,1)S(1)} %get-tuple-element.10.own.feats, f32[256,128]{1,0:T(8,128)S(1)} %get-tuple-element.11.cot, bf16[1024,128]{1,0:T(8,128)(2,1)S(1)} %copy-done, bf16[1024,128]{1,0:T(8,128)(2,1)S(1)} %bitcast.24), custom_call_target="tpu_custom_call" | custom-call | tf_op jit(solution)/shard_map/feature_grads/pallas_call | solution.py:196
  21.3 0.1 copy.21
  21.4 0.7 %convert_element_type.27 = bf16[2,4096]{1,0:T(2,128)(2,1)} reshape(bf16[2,128,32]{2,1,0:T(8,128)(2,1)S(1)} %bitcast.27) | data formatting | bytes 32768 | tf_op jit(solution)/shard_map/convert_element_type | solution.py:220
  22.2 0.1 copy.22
  22.3 0.7 %convert_element_type.31 = bf16[2,4096]{1,0:T(2,128)(2,1)} reshape(bf16[2,128,32]{2,1,0:T(8,128)(2,1)S(1)} %bitcast.28) | data formatting | bytes 32768 | tf_op jit(solution)/shard_map/convert_element_type | solution.py:220
  23.0 0.0 collective-permute-done.3.other
  23.0 0.0 copy-start.1
  23.0 0.7 %copy-done.1 = f32[128]{0:T(128)S(1)} copy-done((f32[128]{0:T(128)S(1)}, f32[128]{0:T(128)}, u32[]{:S(2)}) %copy-start.1) | copy-done | bytes 536
  23.7 3.4 %outer_mean.1 = (f32[8,2,128]{2,1,0:T(2,128)}, f32[1024,128]{1,0:T(8,128)}) custom-call(s32[3]{0:T(128)S(1)} %pad_add_fusion.where, bf16[1024,128]{1,0:T(8,128)(2,1)S(1)} %get-tuple-element.10.own.feats, bf16[1024,128]{1,0:T(8,128)(2,1)S(1)} %collective-permute-done.3.other, f32[256,128]{1,0:T(8,128)S(1)} %get-tuple-element.11.cot, ...), custom_call_target="tpu_custom_call" | custom-call | tf_op jit(solution)/shard_map/outer_mean/pallas_call | solution.py:206
  (5 shorter events, 0.0 us)
Async XLA Ops:
  0.6 0.7 %copy-start.2 = (bf16[2,4096]{1,0:T(2,128)(2,1)S(1)}, bf16[2,4096]{1,0:T(2,128)(2,1)}, u32[]{:S(2)}) copy-start(bf16[2,4096]{1,0:T(2,128)(2,1)} %param.6) | copy-start | bytes 49156
  1.5 0.7 %copy-start.3 = (bf16[2,4096]{1,0:T(2,128)(2,1)S(1)}, bf16[2,4096]{1,0:T(2,128)(2,1)}, u32[]{:S(2)}) copy-start(bf16[2,4096]{1,0:T(2,128)(2,1)} %param.5) | copy-start | bytes 49156
  2.4 2.9 %collective-permute-start = (bf16[1,160,128]{2,1,0:T(8,128)(2,1)S(1)}, bf16[1,160,128]{2,1,0:T(8,128)(2,1)S(1)}, u32[]{:S(2)}, u32[]{:S(2)}) collective-permute-start(bf16[1,160,128]{2,1,0:T(8,128)(2,1)S(1)} %maximum_bitcast_fusion), channel_id=1, source_target_pairs={{0,2},{2,0},{4,6},{6,4},{1,3},{3,1},{5,7},{7,5},{8,10},{10,8},{12,... | collective-permute-start | bytes 122888 | tf_op jit(solution)/shard_map/ppermute | solution.py:52
  5.3 14.2 %copy-start = (bf16[1024,128]{1,0:T(8,128)(2,1)S(1)}, bf16[1024,128]{1,0:T(8,128)(2,1)}, u32[]{:S(2)}) copy-start(bf16[1024,128]{1,0:T(8,128)(2,1)} %weight.1) | copy-start | bytes 786436
  5.3 5.0 %collective-permute-start.1 = (bf16[2,160,128]{2,1,0:T(8,128)(2,1)S(1)}, bf16[2,160,128]{2,1,0:T(8,128)(2,1)S(1)}, u32[]{:S(2)}, u32[]{:S(2)}) collective-permute-start(bf16[2,160,128]{2,1,0:T(8,128)(2,1)S(1)} %pad_maximum_fusion.1), channel_id=1, source_target_pairs={{0,4},{2,6},{4,0},{6,2},{1,5},{3,7},{5,1},{7,3},{8,12},{10,14},{12... | collective-permute-start | bytes 245768 | tf_op jit(solution)/shard_map/ppermute | solution.py:52
  10.4 4.2 %collective-permute-start.2 = (bf16[4,160,128]{2,1,0:T(8,128)(2,1)S(1)}, bf16[4,160,128]{2,1,0:T(8,128)(2,1)S(1)}, u32[]{:S(2)}, u32[]{:S(2)}) collective-permute-start(bf16[4,160,128]{2,1,0:T(8,128)(2,1)S(1)} %pad_maximum_fusion.near), channel_id=1, source_target_pairs={{0,8},{8,0},{1,9},{9,1},{2,10},{10,2},{3,11},{11,3},{4,12},{12,4},... | collective-permute-start | bytes 491528 | tf_op jit(solution)/shard_map/ppermute | solution.py:52
  15.3 7.7 %collective-permute-start.3 = (bf16[1024,128]{1,0:T(8,128)(2,1)S(1)}, bf16[1024,128]{1,0:T(8,128)(2,1)S(1)}, u32[]{:S(2)}, u32[]{:S(2)}) collective-permute-start(bf16[1024,128]{1,0:T(8,128)(2,1)S(1)} %get-tuple-element.10.own.feats), channel_id=1, source_target_pairs={{0,1},{1,0},{2,3},{3,2},{4,5},{5,4},{6,7},{7,6},{8,9},{9,8},{10,11... | collective-permute-start | bytes 786440 | tf_op jit(solution)/shard_map/ppermute | solution.py:52
  23.0 0.7 %copy-start.1 = (f32[128]{0:T(128)S(1)}, f32[128]{0:T(128)}, u32[]{:S(2)}) copy-start(f32[128]{0:T(128)} %param.8) | copy-start | bytes 1540

commit v2 on v0

--- a/solution.py
+++ b/solution.py
@@ -1,13 +1,21 @@
+import functools
+
 import jax
 import jax.numpy as jnp
 from jax import lax
+from jax.experimental import pallas as pl
+from jax.experimental.pallas import tpu as pltpu
 from jax.sharding import PartitionSpec as P
 
 C = 32
 S = 256
-
-
-def on_device(left_features, right_features, weight, bias, cotangent):
+LANES = 128
+F32 = jnp.float32
+BF16 = jnp.bfloat16
+NT = (((1,), (1,)), ((), ()))
+
+
+def tile_plan(left_features, right_features, weight, bias, cotangent):
     left_rows = lax.all_gather(left_features, "col", axis=0, tiled=True)
     right_rows = lax.all_gather(right_features, "row", axis=0, tiled=True)
     row_count = left_rows.shape[0]
@@ -40,7 +48,318 @@
     return (pair_out, left_sum.astype(jnp.bfloat16), right_sum.astype(jnp.bfloat16), weight_grad)
 
 
+def exchange(x, axis, flip, size):
+    return lax.ppermute(x, axis, [(k, k ^ flip) for k in range(size)])
+
+
+def swap_blocks(blocks, width):
+    count = len(blocks)
+    lane_block = lax.broadcasted_iota(jnp.int32, blocks[0].shape, 1) // width
+    bit = 1
+    while bit < count:
+        upper = (lane_block & bit) != 0
+        out = list(blocks)
+        for a in range(count):
+            if a & bit == 0:
+                low, high = blocks[a], blocks[a | bit]
+                out[a] = jnp.where(upper, pltpu.roll(high, bit * width, 1), low)
+                out[a | bit] = jnp.where(upper, high, pltpu.roll(low, LANES - bit * width, 1))
+        blocks = out
+        bit *= 2
+    return blocks
+
+
+def block_kernel(left_in, right_in, cotangent_in, block, left, right, cotangent, scratch, sems):
+    pairs = ((left_in, left), (right_in, right), (cotangent_in, cotangent))
+    copies = [pltpu.make_async_copy(source, into, sems.at[k]) for k, (source, into) in enumerate(pairs)]
+    for copy in copies:
+        copy.start()
+    for copy in copies:
+        copy.wait()
+    held, width = left.shape
+    groups = width // LANES
+    for at, ref in ((0, left), (held * groups, right)):
+        for g in range(groups):
+            scratch[pl.ds(at + g, held, stride=groups), :] = ref[:, g * LANES:(g + 1) * LANES].astype(F32)
+    turned = scratch[...].T
+    rows = swap_blocks([turned[k * C:(k + 1) * C, :] for k in range(LANES // C)], C)
+    block[0, :LANES, :] = jnp.concatenate(rows, axis=0).astype(BF16)
+    per_row, per_col, _ = cotangent.shape
+    cot = cotangent[...].astype(F32)
+    parts = [cot[:, j, :] for j in range(per_col)]
+    block[0, LANES:, :] = jnp.concatenate(parts, axis=0).astype(BF16)
+
+
+def turn_back(rows, scratch, left_grad, right_grad):
+    held, width = left_grad.shape
+    groups = width // LANES
+    blocks = swap_blocks([rows[k * C:(k + 1) * C, :] for k in range(LANES // C)], C)
+    scratch[...] = jnp.concatenate(blocks, axis=0).T
+    for at, ref in ((0, left_grad), (held * groups, right_grad)):
+        for g in range(groups):
+            ref[:, g * LANES:(g + 1) * LANES] = scratch[pl.ds(at + g, held, stride=groups), :].astype(BF16)
+
+
+def spread(source, col, slots, first, into, stride):
+    for slot in range(slots):
+        for t in range(2):
+            at = (col ^ slot) * 2 + t
+            into[pl.ds(at, C, stride=stride), :] = source[slot, first + t * C:first + (t + 1) * C, :].astype(F32)
+
+
+def spread_cot(source, col, slots, rows, into):
+    per_row = 2 * slots
+    for slot in range(slots):
+        cot = source[slot, 4 * C:, :].astype(F32)
+        for j in range(2 * rows):
+            at = pl.multiple_of(((col ^ slot) * 2 + j % 2) * per_row, per_row)
+            into[j // 2, pl.ds(at, per_row), :] = cot[j * per_row:(j + 1) * per_row, :]
+
+
+def mixing_rows(outer_weight, cot_rows):
+    tokens = cot_rows[0].shape[0]
+    copies = LANES // tokens
+    repeated = jnp.concatenate([jnp.concatenate([rows] * copies, axis=0) for rows in cot_rows], axis=0).astype(BF16)
+    grads = lax.dot_general(outer_weight, repeated, NT, preferred_element_type=F32)
+    copy_of = lax.broadcasted_iota(jnp.int32, (C, LANES), 1) // tokens
+    out = []
+    for two in range(2):
+        lanes = grads[:, two * LANES:(two + 1) * LANES]
+        parts = []
+        for group in range(C // copies):
+            first = group * copies * C
+            part = lanes[first:first + C, :]
+            for k in range(1, copies):
+                at = first + k * C
+                part = jnp.where(copy_of == k, lanes[at:at + C, :], part)
+            parts.append((part * (1.0 / S)).astype(BF16))
+        out.append(jnp.concatenate(parts, axis=1))
+    return jnp.concatenate(out, axis=0)
+
+
+def left_cots(cot, half, col, slots):
+    per_row = 2 * slots
+    return [cot[half, pl.ds(col * 2 + t, per_row, stride=per_row), :] for t in range(2)]
+
+
+def right_cots(cot, half, col, slots):
+    per_row = 2 * slots
+    return [cot[half, pl.ds(pl.multiple_of((col * 2 + t) * per_row, per_row), per_row), :] for t in range(2)]
+
+
+def near_kernel(rows, near, weight, bias, lefts, cot, grads, far_mix, weight_t, bias_out, spread_right, weight_dc):
+    slots = near.shape[0]
+    row, col = lax.axis_index("row"), lax.axis_index("col")
+    tokens = 2 * slots
+    spread(near, col, slots, 0, lefts, tokens)
+    spread(near, col, slots, 2 * C, spread_right, tokens)
+    spread_cot(near, col, slots, rows, cot)
+    all_weight = weight[...]
+    weight_dc[...] = jnp.swapaxes(all_weight.astype(F32).reshape(C, C, LANES), 0, 1).reshape(C * C, LANES).astype(BF16)
+    weight_t[...] = all_weight.astype(F32).T.astype(BF16)
+    bias_out[...] = bias[...]
+    mix = mixing_rows(weight_dc[...], left_cots(cot, row, col, slots))
+    grads[:2 * C, :] = jnp.dot(mix, spread_right[...].astype(BF16), preferred_element_type=F32)
+    far_mix[...] = mixing_rows(weight_dc[...], left_cots(cot, 1 - row, col, slots))
+    mix = mixing_rows(all_weight, right_cots(cot, row, col, slots))
+    grads[2 * C:, :] = jnp.dot(mix, lefts[...].astype(BF16), preferred_element_type=F32)
+
+
+def far_kernel(
+    rows, far, near, other_near, near_lefts, near_grads, far_mix, weight,
+    lefts, all_near_lefts, near_rights, cot, left_grad, right_grad, spread_right, turned,
+):
+    slots = far.shape[0]
+    row, col, rep = lax.axis_index("row"), lax.axis_index("col"), lax.axis_index("rep")
+    tokens = 2 * slots
+    all_near_lefts[rep] = near_lefts[...]
+    spread(other_near, col, slots, 0, all_near_lefts.at[1 - rep], tokens)
+    for slot in range(slots):
+        near_rights[rep, col ^ slot] = near[slot, 2 * C:4 * C, :]
+        near_rights[1 - rep, col ^ slot] = other_near[slot, 2 * C:4 * C, :]
+    spread(far, col, slots, 0, lefts, tokens)
+    spread(far, col, slots, 2 * C, spread_right, tokens)
+    spread_cot(far, col, slots, rows, cot)
+    left = jnp.dot(far_mix[...], spread_right[...].astype(BF16), preferred_element_type=F32)
+    mix = mixing_rows(weight[...], right_cots(cot, row, col, slots))
+    right = jnp.dot(mix, lefts[...].astype(BF16), preferred_element_type=F32)
+    turn_back(near_grads[...] + jnp.concatenate([left, right], axis=0), turned, left_grad, right_grad)
+
+
+def outer_kernel(
+    rows, near_lefts, near_rights, near_cot, far_lefts_own, far_cot, far, other, weight_t, bias, left_in, right_in,
+    pair_out, left_out, right_out, weight_out, far_lefts, far_rights, pair_scratch, pair_block, weight_grad, sems,
+):
+    slots = far.shape[0]
+    row, col, rep = lax.axis_index("row"), lax.axis_index("col"), lax.axis_index("rep")
+    copies = [
+        pltpu.make_async_copy(left_in, left_out, sems.at[0]),
+        pltpu.make_async_copy(right_in, right_out, sems.at[1]),
+    ]
+    for copy in copies:
+        copy.start()
+    per_row, per_col = 2 * slots, 2 * rows
+    tokens = rows * per_row
+    far_lefts[rep] = far_lefts_own[...]
+    spread(other, col, slots, 0, far_lefts.at[1 - rep], per_row)
+    for slot in range(slots):
+        far_rights[rep, col ^ slot] = far[slot, 2 * C:4 * C, :]
+        far_rights[1 - rep, col ^ slot] = other[slot, 2 * C:4 * C, :]
+    first_row = row == 0
+
+    def ordered(near, far_part):
+        return jnp.concatenate([jnp.where(first_row, near, far_part), jnp.where(first_row, far_part, near)], axis=1)
+
+    lefts, rights = [], []
+    for half in range(2):
+        near = near_lefts[half].reshape(C, per_row, LANES)
+        both = ordered(near, far_lefts[half].reshape(C, per_row, LANES))
+        lefts.append(both.reshape(C * tokens, LANES).astype(BF16))
+        rights.append(ordered(near_rights[half], far_rights[half]).reshape(tokens * C, LANES))
+    left_all, right_all = jnp.concatenate(lefts, axis=1), jnp.concatenate(rights, axis=1)
+    cots = []
+    for q in range(slots):
+        for half in range(rows):
+            at = slice(q * 2 * per_row, (q + 1) * 2 * per_row)
+            near = near_cot[half, at, :].reshape(2, per_row, LANES)
+            cots.append(ordered(near, far_cot[half, at, :].reshape(2, per_row, LANES)).reshape(2 * tokens, LANES))
+    cot_all = jnp.concatenate(cots, axis=0).astype(BF16)
+
+    count = LANES // tokens
+    pair_t = jnp.zeros((LANES, tokens * tokens), F32)
+    for g in range(C // count):
+        left = left_all[g * LANES:(g + 1) * LANES, :]
+        outer = lax.dot_general(right_all, left, NT, preferred_element_type=F32) * (1.0 / S)
+        parts = []
+        for h in range(tokens // count):
+            first = h * count * C
+            blocks = [outer[first + k * C:first + (k + 1) * C, :] for k in range(count)]
+            parts.append(jnp.concatenate(swap_blocks(blocks, tokens), axis=0).astype(BF16))
+        mean = jnp.concatenate(parts, axis=1)
+        at = slice(g * count * C, (g + 1) * count * C)
+        weight_grad[at, :] = jnp.dot(mean, cot_all, preferred_element_type=F32)
+        copy = pltpu.make_async_copy(weight_grad.at[at], weight_out.at[at], sems.at[2 + g])
+        copy.start()
+        copies.append(copy)
+        pair_t += jnp.dot(weight_t[:, at], mean, preferred_element_type=F32)
+    pair_scratch[...] = pair_t.T
+    for j in range(per_col // 2):
+        column = col * per_col + rep * (per_col // 2) + j
+        at = pl.multiple_of(column * tokens + row * per_row, per_row)
+        pair_block[:, j, :] = pair_scratch[pl.ds(at, per_row), :] + bias[...]
+    copy = pltpu.make_async_copy(pair_block, pair_out, sems.at[2 + C // count])
+    copy.start()
+    copies.append(copy)
+    for copy in copies:
+        copy.wait()
+
+
+def gather_plan(rows, cols, left_features, right_features, weight, bias, cotangent):
+    held, width = left_features.shape
+    seqs = width // C
+    tokens = held * rows * cols
+    half_span = tokens // rows * C
+    per_row, per_col, e = cotangent.shape
+    vmem = pl.BlockSpec(memory_space=pltpu.VMEM)
+    anywhere = pl.BlockSpec(memory_space=pl.ANY)
+    params = pltpu.CompilerParams(vmem_limit_bytes=32 * 1024 * 1024)
+    array = jax.ShapeDtypeStruct
+
+    block = pl.pallas_call(
+        block_kernel,
+        out_shape=array((1, 2 * held * C + per_row * per_col, seqs), BF16),
+        in_specs=[pl.BlockSpec(memory_space=pltpu.HBM)] * 3,
+        out_specs=vmem,
+        scratch_shapes=[
+            pltpu.VMEM((held, width), BF16),
+            pltpu.VMEM((held, width), BF16),
+            pltpu.VMEM((per_row, per_col, e), BF16),
+            pltpu.VMEM((LANES, LANES), F32),
+            pltpu.SemaphoreType.DMA((3,)),
+        ],
+        compiler_params=params,
+        name="own_block",
+    )(*(pltpu.with_memory_space_constraint(x, pltpu.HBM) for x in (left_features, right_features, cotangent)))
+    flip = 1
+    while flip < cols:
+        block = jnp.concatenate([block, exchange(block, "col", flip, cols)], axis=0)
+        flip *= 2
+    far = exchange(block, "row", 1, rows)
+    other_near = exchange(block, "rep", 1, 2)
+    other_far = exchange(far, "rep", 1, 2)
+
+    lefts = array((half_span, seqs), F32)
+    cots = array((rows, cols * held * per_row, e), F32)
+    near_lefts, near_cot, near_grads, far_mix, weight_t, bias_row = pl.pallas_call(
+        functools.partial(near_kernel, rows),
+        out_shape=(
+            lefts,
+            cots,
+            array((2 * held * C, seqs), F32),
+            array((held * C, half_span), BF16),
+            array((e, C * C), BF16),
+            array((1, e), F32),
+        ),
+        in_specs=[vmem] * 3,
+        out_specs=(vmem,) * 6,
+        scratch_shapes=[pltpu.VMEM((half_span, seqs), F32), pltpu.VMEM((C * C, e), BF16)],
+        compiler_params=params,
+        cost_estimate=pl.CostEstimate(flops=300_000_000, bytes_accessed=2_000_000, transcendentals=0),
+        name="near_part",
+    )(block, weight, bias.reshape(1, e))
+
+    far_lefts, both_near_lefts, near_rights, far_cot, left_grad, right_grad = pl.pallas_call(
+        functools.partial(far_kernel, rows),
+        out_shape=(
+            lefts,
+            array((2, half_span, seqs), F32),
+            array((2, cols, 2 * C, seqs), BF16),
+            cots,
+            array((held, width), BF16),
+            array((held, width), BF16),
+        ),
+        in_specs=[vmem] * 7,
+        out_specs=(vmem,) * 6,
+        scratch_shapes=[pltpu.VMEM((half_span, seqs), F32), pltpu.VMEM((LANES, LANES), F32)],
+        compiler_params=params,
+        cost_estimate=pl.CostEstimate(flops=10_000_000_000, bytes_accessed=1_000_000, transcendentals=0),
+        name="far_part",
+    )(far, block, other_near, near_lefts, near_grads, far_mix, weight)
+
+    return tuple(pl.pallas_call(
+        functools.partial(outer_kernel, rows),
+        out_shape=(
+            array((per_row, per_col // 2, e), F32),
+            array((held, width), BF16),
+            array((held, width), BF16),
+            array((C * C, e), F32),
+        ),
+        in_specs=[vmem] * 11,
+        out_specs=(anywhere,) * 4,
+        scratch_shapes=[
+            pltpu.VMEM((2, half_span, seqs), F32),
+            pltpu.VMEM((2, cols, 2 * C, seqs), BF16),
+            pltpu.VMEM((tokens * tokens, e), F32),
+            pltpu.VMEM((per_row, per_col // 2, e), F32),
+            pltpu.VMEM((C * C, e), F32),
+            pltpu.SemaphoreType.DMA((3 + C * tokens // LANES,)),
+        ],
+        compiler_params=params,
+        name="outer_mean",
+    )(both_near_lefts, near_rights, near_cot, far_lefts, far_cot, far, other_far, weight_t, bias_row, left_grad, right_grad))
+
+
 def solution(mesh):
+    rows, cols = mesh.shape["row"], mesh.shape["col"]
+
+    def on_device(left_features, right_features, weight, bias, cotangent):
+        held, width = left_features.shape
+        tokens = held * rows * cols
+        small = held == 2 and rows == 2 and cols & (cols - 1) == 0 and LANES % tokens == 0 and tokens == 16
+        if small and width == LANES * C and weight.shape[1] == LANES and C % (LANES // tokens) == 0:
+            return gather_plan(rows, cols, left_features, right_features, weight, bias, cotangent)
+        return tile_plan(left_features, right_features, weight, bias, cotangent)
+
     in_specs = (
         P(("groups", "row", "col"), "rep"),
         P(("groups", "col", "row"), "rep"),

time: 135 us -> 22.3 us (0.17)
  blocking collectives: 50.4 us -> 0 us
  waiting for transfers between devices: 55.6 us -> 7.35 us
  between operations: 16.9 us -> 0.69 us
  local copies, waits for them, and re-layouts: 8.2 us -> 0.01 us
  starting transfers between devices: 0.08 us -> 8.08 us
  Pallas kernels: 0 us -> 5.83 us
  matrix products: 2.74 us -> 0 us
    psum x1 -> x0, waiting for transfers between devices: 55.6 us -> none  [on_device(): weight_grad = lax.psum(weight_part, ('row', 'col', 'rep'))]
    unnamed x2 -> x0, blocking collectives: 30.8 us -> none
    all_gather x2 -> x0, blocking collectives: 19.6 us -> none  [the longest x1 13.9 us: on_device(): left_rows = lax.all_gather(left_features, 'col', axis=0, tiled=True)]
    ppermute x0 -> x5, starting transfers between devices: none -> 8.08 us  [exchange(): return lax.ppermute(x, axis, [(k, k ^ flip) for k in range(size)])]
    ppermute x0 -> x5, waiting for transfers between devices: none -> 7.35 us  [exchange(): return lax.ppermute(x, axis, [(k, k ^ flip) for k in range(size)])]
    pallas_call x0 -> x4, Pallas kernels: none -> 5.83 us  [the longest x1 2.86 us: gather_plan(): pl.pallas_call(functools.partial(outer_kernel, rows), out_shape=(array((p...]
    unnamed x16 -> x4, local copies, waits for them, and re-layouts: 4.81 us -> 0.01 us
    dot_general x6 -> x0, matrix products: 2.74 us -> none  [the longest x1 1.05 us: on_device(): jnp.einsum('pk,pe->ke', half_mean, flat_grad, preferred_element_type=jnp....]
  transfers between devices with their start and end apart: 2 -> 5, of which waited for: 1 -> 4; matrix products, arithmetic and copies ran while one was open for 5% -> 0% of each run, Pallas kernels for 0% -> 9%
where the time goes in v2:
time: 22.3 us; the launch traced here: 22 us
  starting transfers between devices  8.08 us (36%)
  waiting for transfers between devices  7.35 us (33%)
  Pallas kernels  5.83 us (26%)
  between operations  0.69 us (3%)
    ppermute x5, starting transfers between devices, exchange(): return lax.ppermute(x, axis, [(k, k ^ flip) for k in range(size)])  8.08 us
    ppermute x5, waiting for transfers between devices, exchange(): return lax.ppermute(x, axis, [(k, k ^ flip) for k in range(size)])  7.35 us
    pallas_call x1, Pallas kernels, gather_plan(): pl.pallas_call(functools.partial(outer_kernel, rows), out_shape=(array((p...  2.86 us
    pallas_call x1, Pallas kernels, gather_plan(): pl.pallas_call(functools.partial(near_kernel, rows), out_shape=(lefts, co...  1.14 us
    pallas_call x1, Pallas kernels, gather_plan(): pl.pallas_call(block_kernel, out_shape=array((1, 2 * held * C + per_row *...  1.05 us
    pallas_call x1, Pallas kernels, gather_plan(): pl.pallas_call(functools.partial(far_kernel, rows), out_shape=(lefts, arr...  0.77 us
  transfers between devices with their start and end apart: 5, of which 4 were waited for; matrix products, arithmetic and copies ran while one was open for 0% of the time, Pallas kernels for 9%

profile of v2, /device:TPU:0, one launch (start us, length us, event | category | flops | bytes accessed | tf_op | source)
XLA Modules:
  0.0 22.0 jit_solution(9642261850237439901)
XLA Ops:
  0.6 1.1 %own_block.1 = bf16[1,160,128]{2,1,0:T(8,128)(2,1)S(1)} custom-call(bf16[2,4096]{1,0:T(2,128)(2,1)} %left_in.1, bf16[2,4096]{1,0:T(2,128)(2,1)} %right_in.1, bf16[8,4,128]{2,1,0:T(4,128)(2,1)} %cotangent_in.1), custom_call_target="tpu_custom_call" | custom-call | tf_op jit(solution)/shard_map/own_block/pallas_call | solution.py:268
  1.7 0.0 copy-start
  1.7 3.1 %collective-permute-start = (bf16[1,160,128]{2,1,0:T(8,128)(2,1)S(1)}, bf16[1,160,128]{2,1,0:T(8,128)(2,1)S(1)}, u32[]{:S(2)}, u32[]{:S(2)}) collective-permute-start(bf16[1,160,128]{2,1,0:T(8,128)(2,1)S(1)} %own_block.1), channel_id=1, source_target_pairs={{0,2},{2,0},{4,6},{6,4},{1,3},{3,1},{5,7},{7,5},{8,10},{10,8},{12,... | collective-permute-start | bytes 122888 | tf_op jit(solution)/shard_map/ppermute | solution.py:52
  4.8 2.0 %collective-permute-done = bf16[1,160,128]{2,1,0:T(8,128)(2,1)S(1)} collective-permute-done((bf16[1,160,128]{2,1,0:T(8,128)(2,1)S(1)}, bf16[1,160,128]{2,1,0:T(8,128)(2,1)S(1)}, u32[]{:S(2)}, u32[]{:S(2)}) %collective-permute-start) | collective-permute-done | bytes 40992 | tf_op jit(solution)/shard_map/ppermute | solution.py:52
  6.8 3.1 %collective-permute-start.1 = (bf16[2,160,128]{2,1,0:T(8,128)(2,1)S(1)}, bf16[2,160,128]{2,1,0:T(8,128)(2,1)S(1)}, u32[]{:S(2)}, u32[]{:S(2)}) collective-permute-start(bf16[2,160,128]{2,1,0:T(8,128)(2,1)S(1)} %pad_maximum_fusion.1), channel_id=1, source_target_pairs={{0,4},{2,6},{4,0},{6,2},{1,5},{3,7},{5,1},{7,3},{8,12},{10,14},{12... | collective-permute-start | bytes 245768 | tf_op jit(solution)/shard_map/ppermute | solution.py:52
  9.9 2.4 %collective-permute-done.1 = bf16[2,160,128]{2,1,0:T(8,128)(2,1)S(1)} collective-permute-done((bf16[2,160,128]{2,1,0:T(8,128)(2,1)S(1)}, bf16[2,160,128]{2,1,0:T(8,128)(2,1)S(1)}, u32[]{:S(2)}, u32[]{:S(2)}) %collective-permute-start.1) | collective-permute-done | bytes 81952 | tf_op jit(solution)/shard_map/ppermute | solution.py:52
  12.3 0.0 copy-start.1
  12.3 1.9 %collective-permute-start.2 = (bf16[4,160,128]{2,1,0:T(8,128)(2,1)S(1)}, bf16[4,160,128]{2,1,0:T(8,128)(2,1)S(1)}, u32[]{:S(2)}, u32[]{:S(2)}) collective-permute-start(bf16[4,160,128]{2,1,0:T(8,128)(2,1)S(1)} %pad_maximum_fusion.near), channel_id=1, source_target_pairs={{0,8},{8,0},{1,9},{9,1},{2,10},{10,2},{3,11},{11,3},{4,12},{12,4},... | collective-permute-start | bytes 491528 | tf_op jit(solution)/shard_map/ppermute | solution.py:52
  14.2 0.0 collective-permute-start.3
  14.2 0.0 copy-done
  14.2 0.0 copy-done.1
  14.2 1.1 %near_part.1 = (f32[256,128]{1,0:T(8,128)S(1)}, f32[2,64,128]{2,1,0:T(8,128)S(1)}, f32[128,128]{1,0:T(8,128)S(1)}, bf16[64,256]{1,0:T(8,128)(2,1)S(1)}, bf16[128...) custom-call(bf16[4,160,128]{2,1,0:T(8,128)(2,1)S(1)} %pad_maximum_fusion.near, bf16[1024,128]{1,0:T(8,128)(2,1)S(1)} %copy-done, ...), custom_call_target="tpu_custom_call" | custom-call | flops 300000000 | bytes 2000000 | tf_op jit(solution)/shard_map/near_part/pallas_call | solution.py:293
  15.4 2.3 %collective-permute-done.2.far = bf16[4,160,128]{2,1,0:T(8,128)(2,1)S(1)} collective-permute-done((bf16[4,160,128]{2,1,0:T(8,128)(2,1)S(1)}, bf16[4,160,128]{2,1,0:T(8,128)(2,1)S(1)}, u32[]{:S(2)}, u32[]{:S(2)}) %collective-permute-start.2) | collective-permute-done | bytes 163872 | tf_op jit(solution)/shard_map/ppermute | solution.py:52
  17.7 0.0 collective-permute-start.4
  17.7 0.0 collective-permute-done.3.other_near
  17.7 0.8 %far_part.1 = (f32[256,128]{1,0:T(8,128)S(1)}, f32[2,256,128]{2,1,0:T(8,128)S(1)}, bf16[2,4,64,128]{3,2,1,0:T(8,128)(2,1)S(1)}, f32[2,64,128]{2,1,0:T(8,128)S(1)...) custom-call(bf16[4,160,128]{2,1,0:T(8,128)(2,1)S(1)} %collective-permute-done.2.far, ...), custom_call_target="tpu_custom_call" | custom-call | flops 10000000000 | bytes 1000000 | tf_op jit(solution)/shard_map/far_part/pallas_call | solution.py:311
  18.5 0.6 %collective-permute-done.4.other = bf16[4,160,128]{2,1,0:T(8,128)(2,1)S(1)} collective-permute-done((bf16[4,160,128]{2,1,0:T(8,128)(2,1)S(1)}, bf16[4,160,128]{2,1,0:T(8,128)(2,1)S(1)}, u32[]{:S(2)}, u32[]{:S(2)}) %collective-permute-start.4) | collective-permute-done | bytes 163872 | tf_op jit(solution)/shard_map/ppermute | solution.py:52
  19.1 2.9 %outer_mean.1 = (f32[8,2,128]{2,1,0:T(2,128)}, bf16[2,4096]{1,0:T(2,128)(2,1)}, bf16[2,4096]{1,0:T(2,128)(2,1)}, f32[1024,128]{1,0:T(8,128)}) custom-call(f32[2,256,128]{2,1,0:T(8,128)S(1)} %get-tuple-element.19.near_lefts, bf16[2,4,64,128]{3,2,1,0:T(8,128)(2,1)S(1)} %get-tuple-element.20.near_rights, f32[2,64,128]{2,1,0:T(8,128)S(1)} %get-tuple-element.21.near_cot, ...), custom_call_target="tpu_custom_call" | custom-call | tf_op jit(solution)/shard_map/outer_mean/pallas_call | solution.py:329
  (2 shorter events, 0.0 us)
Async XLA Ops:
  1.7 12.5 %copy-start = (bf16[1024,128]{1,0:T(8,128)(2,1)S(1)}, bf16[1024,128]{1,0:T(8,128)(2,1)}, u32[]{:S(2)}) copy-start(bf16[1024,128]{1,0:T(8,128)(2,1)} %weight.3) | copy-start | bytes 786436
  1.7 5.1 %collective-permute-start = (bf16[1,160,128]{2,1,0:T(8,128)(2,1)S(1)}, bf16[1,160,128]{2,1,0:T(8,128)(2,1)S(1)}, u32[]{:S(2)}, u32[]{:S(2)}) collective-permute-start(bf16[1,160,128]{2,1,0:T(8,128)(2,1)S(1)} %own_block.1), channel_id=1, source_target_pairs={{0,2},{2,0},{4,6},{6,4},{1,3},{3,1},{5,7},{7,5},{8,10},{10,8},{12,... | collective-permute-start | bytes 122888 | tf_op jit(solution)/shard_map/ppermute | solution.py:52
  6.8 5.5 %collective-permute-start.1 = (bf16[2,160,128]{2,1,0:T(8,128)(2,1)S(1)}, bf16[2,160,128]{2,1,0:T(8,128)(2,1)S(1)}, u32[]{:S(2)}, u32[]{:S(2)}) collective-permute-start(bf16[2,160,128]{2,1,0:T(8,128)(2,1)S(1)} %pad_maximum_fusion.1), channel_id=1, source_target_pairs={{0,4},{2,6},{4,0},{6,2},{1,5},{3,7},{5,1},{7,3},{8,12},{10,14},{12... | collective-permute-start | bytes 245768 | tf_op jit(solution)/shard_map/ppermute | solution.py:52
  12.3 1.9 %copy-start.1 = (f32[128]{0:T(128)S(1)}, f32[128]{0:T(128)}, u32[]{:S(2)}) copy-start(f32[128]{0:T(128)} %param.8) | copy-start | bytes 1540
  12.3 5.4 %collective-permute-start.2 = (bf16[4,160,128]{2,1,0:T(8,128)(2,1)S(1)}, bf16[4,160,128]{2,1,0:T(8,128)(2,1)S(1)}, u32[]{:S(2)}, u32[]{:S(2)}) collective-permute-start(bf16[4,160,128]{2,1,0:T(8,128)(2,1)S(1)} %pad_maximum_fusion.near), channel_id=1, source_target_pairs={{0,8},{8,0},{1,9},{9,1},{2,10},{10,2},{3,11},{11,3},{4,12},{12,4},... | collective-permute-start | bytes 491528 | tf_op jit(solution)/shard_map/ppermute | solution.py:52
  14.2 3.5 %collective-permute-start.3 = (bf16[4,160,128]{2,1,0:T(8,128)(2,1)S(1)}, bf16[4,160,128]{2,1,0:T(8,128)(2,1)S(1)}, u32[]{:S(2)}, u32[]{:S(2)}) collective-permute-start(bf16[4,160,128]{2,1,0:T(8,128)(2,1)S(1)} %pad_maximum_fusion.near), channel_id=1, source_target_pairs={{0,1},{1,0},{2,3},{3,2},{4,5},{5,4},{6,7},{7,6},{8,9},{9,8},{10,11... | collective-permute-start | bytes 491528 | tf_op jit(solution)/shard_map/ppermute | solution.py:52
  17.7 1.4 %collective-permute-start.4 = (bf16[4,160,128]{2,1,0:T(8,128)(2,1)S(1)}, bf16[4,160,128]{2,1,0:T(8,128)(2,1)S(1)}, u32[]{:S(2)}, u32[]{:S(2)}) collective-permute-start(bf16[4,160,128]{2,1,0:T(8,128)(2,1)S(1)} %collective-permute-done.2.far), channel_id=1, source_target_pairs={{0,1},{1,0},{2,3},{3,2},{4,5},{5,4},{6,7},{7,6},{8,9},{9,8},{10,11... | collective-permute-start | bytes 491528 | tf_op jit(solution)/shard_map/ppermute | solution.py:52

commit v3 on v2

--- a/solution.py
+++ b/solution.py
@@ -69,8 +69,20 @@
     return blocks
 
 
-def block_kernel(left_in, right_in, cotangent_in, block, left, right, cotangent, scratch, sems):
-    pairs = ((left_in, left), (right_in, right), (cotangent_in, cotangent))
+def skew_blocks(blocks, width):
+    count = len(blocks)
+    lane_block = lax.broadcasted_iota(jnp.int32, blocks[0].shape, 1) // width
+    blocks = [pltpu.roll(x, k * width, 1) if k else x for k, x in enumerate(blocks)]
+    bit = 1
+    while bit < count:
+        upper = (lane_block & bit) != 0
+        blocks = [jnp.where(upper, blocks[(m + bit) % count], blocks[m]) for m in range(count)]
+        bit *= 2
+    return [blocks[-c % count] for c in range(count)]
+
+
+def block_kernel(left_in, right_in, cotangent_in, bias_in, block, bias, left, right, cotangent, scratch, sems):
+    pairs = ((left_in, left), (right_in, right), (cotangent_in, cotangent), (bias_in, bias))
     copies = [pltpu.make_async_copy(source, into, sems.at[k]) for k, (source, into) in enumerate(pairs)]
     for copy in copies:
         copy.start()
@@ -147,7 +159,7 @@
     return [cot[half, pl.ds(pl.multiple_of((col * 2 + t) * per_row, per_row), per_row), :] for t in range(2)]
 
 
-def near_kernel(rows, near, weight, bias, lefts, cot, grads, far_mix, weight_t, bias_out, spread_right, weight_dc):
+def near_kernel(rows, near, weight, lefts, cot, grads, far_mix, spread_right, weight_dc):
     slots = near.shape[0]
     row, col = lax.axis_index("row"), lax.axis_index("col")
     tokens = 2 * slots
@@ -156,8 +168,6 @@
     spread_cot(near, col, slots, rows, cot)
     all_weight = weight[...]
     weight_dc[...] = jnp.swapaxes(all_weight.astype(F32).reshape(C, C, LANES), 0, 1).reshape(C * C, LANES).astype(BF16)
-    weight_t[...] = all_weight.astype(F32).T.astype(BF16)
-    bias_out[...] = bias[...]
     mix = mixing_rows(weight_dc[...], left_cots(cot, row, col, slots))
     grads[:2 * C, :] = jnp.dot(mix, spread_right[...].astype(BF16), preferred_element_type=F32)
     far_mix[...] = mixing_rows(weight_dc[...], left_cots(cot, 1 - row, col, slots))
@@ -165,32 +175,50 @@
     grads[2 * C:, :] = jnp.dot(mix, lefts[...].astype(BF16), preferred_element_type=F32)
 
 
+def ordered(first, near, far):
+    return jnp.concatenate([jnp.where(first, near, far), jnp.where(first, far, near)], axis=1)
+
+
 def far_kernel(
-    rows, far, near, other_near, near_lefts, near_grads, far_mix, weight,
-    lefts, all_near_lefts, near_rights, cot, left_grad, right_grad, spread_right, turned,
+    rows, far, near, near_lefts, near_cot, near_grads, far_mix, weight,
+    lefts, rights, cot_all, left_grad, right_grad, far_lefts, far_cot, spread_right, turned,
 ):
     slots = far.shape[0]
-    row, col, rep = lax.axis_index("row"), lax.axis_index("col"), lax.axis_index("rep")
-    tokens = 2 * slots
-    all_near_lefts[rep] = near_lefts[...]
-    spread(other_near, col, slots, 0, all_near_lefts.at[1 - rep], tokens)
-    for slot in range(slots):
-        near_rights[rep, col ^ slot] = near[slot, 2 * C:4 * C, :]
-        near_rights[1 - rep, col ^ slot] = other_near[slot, 2 * C:4 * C, :]
-    spread(far, col, slots, 0, lefts, tokens)
-    spread(far, col, slots, 2 * C, spread_right, tokens)
-    spread_cot(far, col, slots, rows, cot)
+    row, col = lax.axis_index("row"), lax.axis_index("col")
+    per_row = 2 * slots
+    tokens = rows * per_row
+    spread(far, col, slots, 0, far_lefts, per_row)
+    spread(far, col, slots, 2 * C, spread_right, per_row)
+    spread_cot(far, col, slots, rows, far_cot)
     left = jnp.dot(far_mix[...], spread_right[...].astype(BF16), preferred_element_type=F32)
-    mix = mixing_rows(weight[...], right_cots(cot, row, col, slots))
-    right = jnp.dot(mix, lefts[...].astype(BF16), preferred_element_type=F32)
+    mix = mixing_rows(weight[...], right_cots(far_cot, row, col, slots))
+    right = jnp.dot(mix, far_lefts[...].astype(BF16), preferred_element_type=F32)
     turn_back(near_grads[...] + jnp.concatenate([left, right], axis=0), turned, left_grad, right_grad)
+    first = row == 0
+    both = ordered(first, near_lefts[...].reshape(C, per_row, LANES), far_lefts[...].reshape(C, per_row, LANES))
+    lefts[...] = both.reshape(C * tokens, LANES).astype(BF16)
+    sort_rights(near, far, row, col, slots, rows, 2 * C, rights)
+    for q in range(slots):
+        at = slice(q * 2 * per_row, (q + 1) * 2 * per_row)
+        for half in range(rows):
+            near_rows = near_cot[half, at, :].reshape(2, per_row, LANES)
+            both = ordered(first, near_rows, far_cot[half, at, :].reshape(2, per_row, LANES))
+            first_row = (q * rows + half) * 2 * tokens
+            cot_all[first_row:first_row + 2 * tokens, :] = both.reshape(2 * tokens, LANES).astype(BF16)
+
+
+def sort_rights(near, far, row, col, slots, rows, first, into):
+    for half, source in enumerate((near, far)):
+        for slot in range(slots):
+            chip = (col ^ slot) * rows + lax.rem(row + half, rows)
+            into[pl.ds(pl.multiple_of(chip * 2 * C, 2 * C), 2 * C), :] = source[slot, first:first + 2 * C, :]
 
 
 def outer_kernel(
-    rows, near_lefts, near_rights, near_cot, far_lefts_own, far_cot, far, other, weight_t, bias, left_in, right_in,
-    pair_out, left_out, right_out, weight_out, far_lefts, far_rights, pair_scratch, pair_block, weight_grad, sems,
+    rows, own_lefts, own_rights, other, cot_all, weight, bias, left_in, right_in,
+    pair_out, left_out, right_out, weight_out, spread_left, lefts, rights, pair_block, weight_grad, sems,
 ):
-    slots = far.shape[0]
+    slots = other.shape[0] // rows
     row, col, rep = lax.axis_index("row"), lax.axis_index("col"), lax.axis_index("rep")
     copies = [
         pltpu.make_async_copy(left_in, left_out, sems.at[0]),
@@ -200,54 +228,65 @@
         copy.start()
     per_row, per_col = 2 * slots, 2 * rows
     tokens = rows * per_row
-    far_lefts[rep] = far_lefts_own[...]
-    spread(other, col, slots, 0, far_lefts.at[1 - rep], per_row)
-    for slot in range(slots):
-        far_rights[rep, col ^ slot] = far[slot, 2 * C:4 * C, :]
-        far_rights[1 - rep, col ^ slot] = other[slot, 2 * C:4 * C, :]
-    first_row = row == 0
-
-    def ordered(near, far_part):
-        return jnp.concatenate([jnp.where(first_row, near, far_part), jnp.where(first_row, far_part, near)], axis=1)
-
-    lefts, rights = [], []
-    for half in range(2):
-        near = near_lefts[half].reshape(C, per_row, LANES)
-        both = ordered(near, far_lefts[half].reshape(C, per_row, LANES))
-        lefts.append(both.reshape(C * tokens, LANES).astype(BF16))
-        rights.append(ordered(near_rights[half], far_rights[half]).reshape(tokens * C, LANES))
-    left_all, right_all = jnp.concatenate(lefts, axis=1), jnp.concatenate(rights, axis=1)
-    cots = []
-    for q in range(slots):
-        for half in range(rows):
-            at = slice(q * 2 * per_row, (q + 1) * 2 * per_row)
-            near = near_cot[half, at, :].reshape(2, per_row, LANES)
-            cots.append(ordered(near, far_cot[half, at, :].reshape(2, per_row, LANES)).reshape(2 * tokens, LANES))
-    cot_all = jnp.concatenate(cots, axis=0).astype(BF16)
-
+    for half in range(rows):
+        first = lax.rem(row + half, rows) * per_row
+        for slot in range(slots):
+            for t in range(2):
+                at = first + (col ^ slot) * 2 + t
+                block = other[half * slots + slot, t * C:(t + 1) * C, :]
+                spread_left[pl.ds(at, C, stride=tokens), :] = block.astype(F32)
+    lefts[rep] = own_lefts[...]
+    lefts[1 - rep] = spread_left[...].astype(BF16)
+    rights[rep] = own_rights[...]
+    sort_rights(other.at[:slots], other.at[slots:], row, col, slots, rows, 2 * C, rights.at[1 - rep])
+
+    def all_of(ref, at):
+        return jnp.concatenate([ref[0, at, :], ref[1, at, :]], axis=1)
+
+    right_all = all_of(rights, slice(None))
     count = LANES // tokens
-    pair_t = jnp.zeros((LANES, tokens * tokens), F32)
-    for g in range(C // count):
-        left = left_all[g * LANES:(g + 1) * LANES, :]
+    groups = C // count
+    means = [[[] for _ in range(groups)] for _ in range(count)]
+    for g in range(groups):
+        left = all_of(lefts, slice(g * LANES, (g + 1) * LANES))
         outer = lax.dot_general(right_all, left, NT, preferred_element_type=F32) * (1.0 / S)
-        parts = []
         for h in range(tokens // count):
             first = h * count * C
             blocks = [outer[first + k * C:first + (k + 1) * C, :] for k in range(count)]
-            parts.append(jnp.concatenate(swap_blocks(blocks, tokens), axis=0).astype(BF16))
-        mean = jnp.concatenate(parts, axis=1)
-        at = slice(g * count * C, (g + 1) * count * C)
-        weight_grad[at, :] = jnp.dot(mean, cot_all, preferred_element_type=F32)
-        copy = pltpu.make_async_copy(weight_grad.at[at], weight_out.at[at], sems.at[2 + g])
+            for c, mean in enumerate(skew_blocks(blocks, tokens)):
+                means[c][g].append(mean)
+    for c in range(count):
+        mean = jnp.concatenate([jnp.concatenate(halves, axis=1) for halves in means[c]], axis=0).astype(BF16)
+        cot = jnp.concatenate(
+            [
+                cot_all[at:at + tokens, :]
+                for h in range(tokens // count)
+                for at in [(h * count + (k - c) % count) * tokens for k in range(count)]
+            ],
+            axis=0,
+        )
+        part = jnp.dot(mean, cot, preferred_element_type=F32)
+        at = slice(c * C, (c + 1) * C)
+        weight_grad[:, at, :] = part.reshape(groups, C, LANES)
+        copy = pltpu.make_async_copy(weight_grad.at[:, at], weight_out.at[:, at], sems.at[3 + c])
         copy.start()
         copies.append(copy)
-        pair_t += jnp.dot(weight_t[:, at], mean, preferred_element_type=F32)
-    pair_scratch[...] = pair_t.T
-    for j in range(per_col // 2):
-        column = col * per_col + rep * (per_col // 2) + j
-        at = pl.multiple_of(column * tokens + row * per_row, per_row)
-        pair_block[:, j, :] = pair_scratch[pl.ds(at, per_row), :] + bias[...]
-    copy = pltpu.make_async_copy(pair_block, pair_out, sems.at[2 + C // count])
+
+    own_count = per_col // 2
+    at = pl.ds(pl.multiple_of((col * per_col + rep * own_count) * C, own_count * C), own_count * C)
+    own = lax.dot_general(all_of(lefts, slice(None)), all_of(rights, at), NT, preferred_element_type=F32) * (1.0 / S)
+    own_mean = jnp.concatenate(
+        [
+            jnp.concatenate([own[c * tokens:(c + 1) * tokens, t * C:(t + 1) * C] for c in range(C)], axis=1)
+            for t in range(own_count)
+        ],
+        axis=0,
+    ).astype(BF16)
+    own_pairs = jnp.dot(own_mean, weight[...], preferred_element_type=F32) + bias[...]
+    for t in range(own_count):
+        lower = own_pairs[t * tokens:t * tokens + per_row, :]
+        pair_block[:, t, :] = jnp.where(row == 0, lower, own_pairs[t * tokens + per_row:(t + 1) * tokens, :])
+    copy = pltpu.make_async_copy(pair_block, pair_out, sems.at[2])
     copy.start()
     copies.append(copy)
     for copy in copies:
@@ -265,88 +304,95 @@
     params = pltpu.CompilerParams(vmem_limit_bytes=32 * 1024 * 1024)
     array = jax.ShapeDtypeStruct
 
-    block = pl.pallas_call(
+    in_hbm = [left_features, right_features, cotangent, bias.reshape(1, e)]
+    block, bias_row = pl.pallas_call(
         block_kernel,
-        out_shape=array((1, 2 * held * C + per_row * per_col, seqs), BF16),
-        in_specs=[pl.BlockSpec(memory_space=pltpu.HBM)] * 3,
-        out_specs=vmem,
+        out_shape=(array((1, 2 * held * C + per_row * per_col, seqs), BF16), array((1, e), F32)),
+        in_specs=[pl.BlockSpec(memory_space=pltpu.HBM)] * 4,
+        out_specs=(vmem, vmem),
         scratch_shapes=[
             pltpu.VMEM((held, width), BF16),
             pltpu.VMEM((held, width), BF16),
             pltpu.VMEM((per_row, per_col, e), BF16),
             pltpu.VMEM((LANES, LANES), F32),
-            pltpu.SemaphoreType.DMA((3,)),
+            pltpu.SemaphoreType.DMA((4,)),
         ],
         compiler_params=params,
         name="own_block",
-    )(*(pltpu.with_memory_space_constraint(x, pltpu.HBM) for x in (left_features, right_features, cotangent)))
+    )(*(pltpu.with_memory_space_constraint(x, pltpu.HBM) for x in in_hbm))
     flip = 1
     while flip < cols:
-        block = jnp.concatenate([block, exchange(block, "col", flip, cols)], axis=0)
+        arrived = exchange(block, "col", flip, cols)
+        if flip * 2 == cols:
+            far = [exchange(block, "row", 1, rows), exchange(arrived, "row", 1, rows)]
+        block = jnp.concatenate([block, arrived], axis=0)
         flip *= 2
-    far = exchange(block, "row", 1, rows)
-    other_near = exchange(block, "rep", 1, 2)
-    other_far = exchange(far, "rep", 1, 2)
+    far = jnp.concatenate(far, axis=0)
+    other = exchange(jnp.concatenate([block, far], axis=0), "rep", 1, 2)
 
     lefts = array((half_span, seqs), F32)
     cots = array((rows, cols * held * per_row, e), F32)
-    near_lefts, near_cot, near_grads, far_mix, weight_t, bias_row = pl.pallas_call(
+    near_lefts, near_cot, near_grads, far_mix = pl.pallas_call(
         functools.partial(near_kernel, rows),
         out_shape=(
             lefts,
             cots,
             array((2 * held * C, seqs), F32),
             array((held * C, half_span), BF16),
-            array((e, C * C), BF16),
-            array((1, e), F32),
         ),
-        in_specs=[vmem] * 3,
-        out_specs=(vmem,) * 6,
+        in_specs=[vmem] * 2,
+        out_specs=(vmem,) * 4,
         scratch_shapes=[pltpu.VMEM((half_span, seqs), F32), pltpu.VMEM((C * C, e), BF16)],
         compiler_params=params,
         cost_estimate=pl.CostEstimate(flops=300_000_000, bytes_accessed=2_000_000, transcendentals=0),
         name="near_part",
-    )(block, weight, bias.reshape(1, e))
-
-    far_lefts, both_near_lefts, near_rights, far_cot, left_grad, right_grad = pl.pallas_call(
+    )(block, weight)
+
+    own_lefts, own_rights, cot_all, left_grad, right_grad = pl.pallas_call(
         functools.partial(far_kernel, rows),
         out_shape=(
-            lefts,
-            array((2, half_span, seqs), F32),
-            array((2, cols, 2 * C, seqs), BF16),
-            cots,
+            array((tokens * C, seqs), BF16),
+            array((tokens * C, seqs), BF16),
+            array((tokens * tokens, e), BF16),
             array((held, width), BF16),
             array((held, width), BF16),
         ),
         in_specs=[vmem] * 7,
-        out_specs=(vmem,) * 6,
-        scratch_shapes=[pltpu.VMEM((half_span, seqs), F32), pltpu.VMEM((LANES, LANES), F32)],
+        out_specs=(vmem,) * 5,
+        scratch_shapes=[
+            pltpu.VMEM((half_span, seqs), F32),
+            pltpu.VMEM(cots.shape, F32),
+            pltpu.VMEM((half_span, seqs), F32),
+            pltpu.VMEM((LANES, LANES), F32),
+        ],
         compiler_params=params,
         cost_estimate=pl.CostEstimate(flops=10_000_000_000, bytes_accessed=1_000_000, transcendentals=0),
         name="far_part",
-    )(far, block, other_near, near_lefts, near_grads, far_mix, weight)
-
-    return tuple(pl.pallas_call(
+    )(far, block, near_lefts, near_cot, near_grads, far_mix, weight)
+
+    split = (C * tokens // LANES, LANES // tokens * C, e)
+    pair_out, left_grad, right_grad, weight_grad = pl.pallas_call(
         functools.partial(outer_kernel, rows),
         out_shape=(
             array((per_row, per_col // 2, e), F32),
             array((held, width), BF16),
             array((held, width), BF16),
-            array((C * C, e), F32),
+            array(split, F32),
         ),
-        in_specs=[vmem] * 11,
+        in_specs=[vmem] * 8,
         out_specs=(anywhere,) * 4,
         scratch_shapes=[
-            pltpu.VMEM((2, half_span, seqs), F32),
-            pltpu.VMEM((2, cols, 2 * C, seqs), BF16),
-            pltpu.VMEM((tokens * tokens, e), F32),
+            pltpu.VMEM((tokens * C, seqs), F32),
+            pltpu.VMEM((2, tokens * C, seqs), BF16),
+            pltpu.VMEM((2, tokens * C, seqs), BF16),
             pltpu.VMEM((per_row, per_col // 2, e), F32),
-            pltpu.VMEM((C * C, e), F32),
-            pltpu.SemaphoreType.DMA((3 + C * tokens // LANES,)),
+            pltpu.VMEM(split, F32),
+            pltpu.SemaphoreType.DMA((3 + LANES // tokens,)),
         ],
         compiler_params=params,
         name="outer_mean",
-    )(both_near_lefts, near_rights, near_cot, far_lefts, far_cot, far, other_far, weight_t, bias_row, left_grad, right_grad))
+    )(own_lefts, own_rights, other, cot_all, weight, bias_row, left_grad, right_grad)
+    return pair_out, left_grad, right_grad, weight_grad.reshape(C * C, e)
 
 
 def solution(mesh):

time: 22.3 us -> 20.7 us (0.928)
  waiting for transfers between devices: 7.35 us -> 5.09 us
  starting transfers between devices: 8.08 us -> 9.57 us
  Pallas kernels: 5.83 us -> 4.98 us
    ppermute x5, waiting for transfers between devices: 7.35 us -> 5.09 us  [exchange(): return lax.ppermute(x, axis, [(k, k ^ flip) for k in range(size)])]
    ppermute x5, starting transfers between devices: 8.08 us -> 9.57 us  [exchange(): return lax.ppermute(x, axis, [(k, k ^ flip) for k in range(size)])]
    pallas_call x1, Pallas kernels: 2.86 us -> 1.99 us  [gather_plan(): pl.pallas_call(functools.partial(outer_kernel, rows), out_shape=(array((p...]
where the time goes in v3:
time: 20.7 us; the launch traced here: 20.5 us
  starting transfers between devices  9.57 us (46%)
  waiting for transfers between devices  5.09 us (25%)
  Pallas kernels  4.98 us (24%)
  between operations  0.71 us (3%)
    ppermute x5, starting transfers between devices, exchange(): return lax.ppermute(x, axis, [(k, k ^ flip) for k in range(size)])  9.57 us
    ppermute x5, waiting for transfers between devices, exchange(): return lax.ppermute(x, axis, [(k, k ^ flip) for k in range(size)])  5.09 us
    pallas_call x1, Pallas kernels, gather_plan(): pl.pallas_call(functools.partial(outer_kernel, rows), out_shape=(array((p...  1.99 us
    pallas_call x1, Pallas kernels, gather_plan(): pl.pallas_call(functools.partial(near_kernel, rows), out_shape=(lefts, co...  1.13 us
    pallas_call x1, Pallas kernels, gather_plan(): pl.pallas_call(block_kernel, out_shape=(array((1, 2 * held * C + per_row...  1.07 us
    pallas_call x1, Pallas kernels, gather_plan(): pl.pallas_call(functools.partial(far_kernel, rows), out_shape=(array((tok...  0.8 us
  transfers between devices with their start and end apart: 5, of which 4 were waited for; matrix products, arithmetic and copies ran while one was open for 0% of the time, Pallas kernels for 9%

profile of v3, /device:TPU:0, one launch (start us, length us, event | category | flops | bytes accessed | tf_op | source)
XLA Modules:
  0.0 20.5 jit_solution(6117994623632104258)
XLA Ops:
  0.6 1.1 %own_block.1 = (bf16[1,160,128]{2,1,0:T(8,128)(2,1)S(1)}, f32[1,128]{1,0:T(1,128)S(1)}) custom-call(bf16[2,4096]{1,0:T(2,128)(2,1)} %left_in.1, bf16[2,4096]{1,0:T(2,128)(2,1)} %right_in.1, bf16[8,4,128]{2,1,0:T(4,128)(2,1)} %cotangent_in.1, f32[1,128]{1,0:T(1,128)} %bitcast.2), custom_call_target="tpu_custom_call" | custom-call | tf_op jit(solution)/shard_map/own_block/pallas_call | solution.py:308
  1.7 0.0 copy-start
  1.7 3.1 %collective-permute-start = (bf16[1,160,128]{2,1,0:T(8,128)(2,1)S(1)}, bf16[1,160,128]{2,1,0:T(8,128)(2,1)S(1)}, u32[]{:S(2)}, u32[]{:S(2)}) collective-permute-start(bf16[1,160,128]{2,1,0:T(8,128)(2,1)S(1)} %get-tuple-element.19), channel_id=1, source_target_pairs={{0,2},{2,0},{4,6},{6,4},{1,3},{3,1},{5,7},{7,5},{8,10},{10,8},{12,... | collective-permute-start | bytes 122888 | tf_op jit(solution)/shard_map/ppermute | solution.py:52
  4.8 2.0 %collective-permute-done = bf16[1,160,128]{2,1,0:T(8,128)(2,1)S(1)} collective-permute-done((bf16[1,160,128]{2,1,0:T(8,128)(2,1)S(1)}, bf16[1,160,128]{2,1,0:T(8,128)(2,1)S(1)}, u32[]{:S(2)}, u32[]{:S(2)}) %collective-permute-start) | collective-permute-done | bytes 40992 | tf_op jit(solution)/shard_map/ppermute | solution.py:52
  6.8 3.1 %collective-permute-start.2 = (bf16[2,160,128]{2,1,0:T(8,128)(2,1)S(1)}, bf16[2,160,128]{2,1,0:T(8,128)(2,1)S(1)}, u32[]{:S(2)}, u32[]{:S(2)}) collective-permute-start(bf16[2,160,128]{2,1,0:T(8,128)(2,1)S(1)} %get-tuple-element.38), channel_id=1, source_target_pairs={{0,4},{2,6},{4,0},{6,2},{1,5},{3,7},{5,1},{7,3},{8,12},{10,14},{12... | collective-permute-start | bytes 245768 | tf_op jit(solution)/shard_map/ppermute | solution.py:52
  9.9 1.5 %collective-permute-start.1 = (bf16[2,160,128]{2,1,0:T(8,128)(2,1)S(1)}, bf16[2,160,128]{2,1,0:T(8,128)(2,1)S(1)}, u32[]{:S(2)}, u32[]{:S(2)}) collective-permute-start(bf16[2,160,128]{2,1,0:T(8,128)(2,1)S(1)} %get-tuple-element.38), channel_id=1, source_target_pairs={{0,8},{8,0},{1,9},{9,1},{2,10},{10,2},{3,11},{11,3},{4,12},{12,4},... | collective-permute-start | bytes 245768 | tf_op jit(solution)/shard_map/ppermute | solution.py:52
  11.4 0.9 %collective-permute-done.2 = bf16[2,160,128]{2,1,0:T(8,128)(2,1)S(1)} collective-permute-done((bf16[2,160,128]{2,1,0:T(8,128)(2,1)S(1)}, bf16[2,160,128]{2,1,0:T(8,128)(2,1)S(1)}, u32[]{:S(2)}, u32[]{:S(2)}) %collective-permute-start.2) | collective-permute-done | bytes 81952 | tf_op jit(solution)/shard_map/ppermute | solution.py:52
  12.3 1.8 %collective-permute-start.3 = (bf16[2,160,128]{2,1,0:T(8,128)(2,1)S(1)}, bf16[2,160,128]{2,1,0:T(8,128)(2,1)S(1)}, u32[]{:S(2)}, u32[]{:S(2)}) collective-permute-start(bf16[2,160,128]{2,1,0:T(8,128)(2,1)S(1)} %collective-permute-done.2), channel_id=1, source_target_pairs={{0,8},{8,0},{1,9},{9,1},{2,10},{10,2},{3,11},{11,3},{4,12},{12,4},... | collective-permute-start | bytes 245768 | tf_op jit(solution)/shard_map/ppermute | solution.py:52
  14.2 0.0 copy-done
  14.2 1.1 %near_part.1 = (f32[256,128]{1,0:T(8,128)S(1)}, f32[2,64,128]{2,1,0:T(8,128)S(1)}, f32[128,128]{1,0:T(8,128)S(1)}, bf16[64,256]{1,0:T(8,128)(2,1)S(1)}) custom-call(bf16[4,160,128]{2,1,0:T(8,128)(2,1)S(1)} %get-tuple-element.35.near, bf16[1024,128]{1,0:T(8,128)(2,1)S(1)} %copy-done), custom_call_target="tpu_custom_call" | custom-call | flops 300000000 | bytes 2000000 | tf_op jit(solution)/shard_map/near_part/pallas_call | solution.py:335
  15.3 0.0 collective-permute-done.1
  15.4 1.4 %collective-permute-done.3 = bf16[2,160,128]{2,1,0:T(8,128)(2,1)S(1)} collective-permute-done((bf16[2,160,128]{2,1,0:T(8,128)(2,1)S(1)}, bf16[2,160,128]{2,1,0:T(8,128)(2,1)S(1)}, u32[]{:S(2)}, u32[]{:S(2)}) %collective-permute-start.3) | collective-permute-done | bytes 81952 | tf_op jit(solution)/shard_map/ppermute | solution.py:52
  16.8 0.1 collective-permute-start.4
  16.9 0.8 %far_part.1 = (bf16[512,128]{1,0:T(8,128)(2,1)S(1)}, bf16[512,128]{1,0:T(8,128)(2,1)S(1)}, bf16[256,128]{1,0:T(8,128)(2,1)S(1)}, bf16[2,4096]{1,0:T(2,128)(2,1)S(1)}, bf16[2,4096]{1,0:T(2,128)(2,1)S(1)}) custom-call(bf16[4,160,128]{2,1,0:T(8,128)(2,1)S(1)} %pad_maximum_fusion.far, bf16[4,160,128]{2,1,0:T(8,128)(2,1)S(1)} %get-tuple-element.35.near, ...), custom_call_target="tpu_custom_call" | custom-call | flops 10000000000 | bytes 1000000 | tf_op jit(solution)/shard_map/far_part/pallas_call | solution.py:351
  17.7 0.8 %collective-permute-done.4.other = bf16[8,160,128]{2,1,0:T(8,128)(2,1)S(1)} collective-permute-done((bf16[8,160,128]{2,1,0:T(8,128)(2,1)S(1)}, bf16[8,160,128]{2,1,0:T(8,128)(2,1)S(1)}, u32[]{:S(2)}, u32[]{:S(2)}) %collective-permute-start.4) | collective-permute-done | bytes 327712 | tf_op jit(solution)/shard_map/ppermute | solution.py:52
  18.5 2.0 %outer_mean.1 = (f32[8,2,128]{2,1,0:T(2,128)}, bf16[2,4096]{1,0:T(2,128)(2,1)}, bf16[2,4096]{1,0:T(2,128)(2,1)}, f32[4,256,128]{2,1,0:T(8,128)}) custom-call(bf16[512,128]{1,0:T(8,128)(2,1)S(1)} %get-tuple-element.24.own_lefts, bf16[512,128]{1,0:T(8,128)(2,1)S(1)} %get-tuple-element.25.own_rights, bf16[8,160,128]{2,1,0:T(8,128)(2,1)S(1)} %collective-permute-done.4.other, ...), custom_call_target="tpu_custom_call" | custom-call | tf_op jit(solution)/shard_map/outer_mean/pallas_call | solution.py:374
  (6 shorter events, 0.1 us)
Async XLA Ops:
  1.7 12.5 %copy-start = (bf16[1024,128]{1,0:T(8,128)(2,1)S(1)}, bf16[1024,128]{1,0:T(8,128)(2,1)}, u32[]{:S(2)}) copy-start(bf16[1024,128]{1,0:T(8,128)(2,1)} %weight.5) | copy-start | bytes 786436
  1.7 5.1 %collective-permute-start = (bf16[1,160,128]{2,1,0:T(8,128)(2,1)S(1)}, bf16[1,160,128]{2,1,0:T(8,128)(2,1)S(1)}, u32[]{:S(2)}, u32[]{:S(2)}) collective-permute-start(bf16[1,160,128]{2,1,0:T(8,128)(2,1)S(1)} %get-tuple-element.19), channel_id=1, source_target_pairs={{0,2},{2,0},{4,6},{6,4},{1,3},{3,1},{5,7},{7,5},{8,10},{10,8},{12,... | collective-permute-start | bytes 122888 | tf_op jit(solution)/shard_map/ppermute | solution.py:52
  6.8 5.5 %collective-permute-start.2 = (bf16[2,160,128]{2,1,0:T(8,128)(2,1)S(1)}, bf16[2,160,128]{2,1,0:T(8,128)(2,1)S(1)}, u32[]{:S(2)}, u32[]{:S(2)}) collective-permute-start(bf16[2,160,128]{2,1,0:T(8,128)(2,1)S(1)} %get-tuple-element.38), channel_id=1, source_target_pairs={{0,4},{2,6},{4,0},{6,2},{1,5},{3,7},{5,1},{7,3},{8,12},{10,14},{12... | collective-permute-start | bytes 245768 | tf_op jit(solution)/shard_map/ppermute | solution.py:52
  9.9 5.4 %collective-permute-start.1 = (bf16[2,160,128]{2,1,0:T(8,128)(2,1)S(1)}, bf16[2,160,128]{2,1,0:T(8,128)(2,1)S(1)}, u32[]{:S(2)}, u32[]{:S(2)}) collective-permute-start(bf16[2,160,128]{2,1,0:T(8,128)(2,1)S(1)} %get-tuple-element.38), channel_id=1, source_target_pairs={{0,8},{8,0},{1,9},{9,1},{2,10},{10,2},{3,11},{11,3},{4,12},{12,4},... | collective-permute-start | bytes 245768 | tf_op jit(solution)/shard_map/ppermute | solution.py:52
  12.3 4.4 %collective-permute-start.3 = (bf16[2,160,128]{2,1,0:T(8,128)(2,1)S(1)}, bf16[2,160,128]{2,1,0:T(8,128)(2,1)S(1)}, u32[]{:S(2)}, u32[]{:S(2)}) collective-permute-start(bf16[2,160,128]{2,1,0:T(8,128)(2,1)S(1)} %collective-permute-done.2), channel_id=1, source_target_pairs={{0,8},{8,0},{1,9},{9,1},{2,10},{10,2},{3,11},{11,3},{4,12},{12,4},... | collective-permute-start | bytes 245768 | tf_op jit(solution)/shard_map/ppermute | solution.py:52
  16.8 1.7 %collective-permute-start.4 = (bf16[8,160,128]{2,1,0:T(8,128)(2,1)S(1)}, bf16[8,160,128]{2,1,0:T(8,128)(2,1)S(1)}, u32[]{:S(2)}, u32[]{:S(2)}) collective-permute-start(bf16[8,160,128]{2,1,0:T(8,128)(2,1)S(1)} %constant_dynamic-update-slice_fusion.5), channel_id=1, source_target_pairs={{0,1},{1,0},{2,3},{3,2},{4,5},{5,4},{6,7},{7,6},{8,9},{9,8},{10,11... | collective-permute-start | bytes 983048 | tf_op jit(solution)/shard_map/ppermute | solution.py:52

commit v4 on v3

--- a/solution.py
+++ b/solution.py
@@ -90,9 +90,7 @@
         copy.wait()
     held, width = left.shape
     groups = width // LANES
-    for at, ref in ((0, left), (held * groups, right)):
-        for g in range(groups):
-            scratch[pl.ds(at + g, held, stride=groups), :] = ref[:, g * LANES:(g + 1) * LANES].astype(F32)
+    scratch[...] = jnp.concatenate([ref[...].astype(F32).reshape(held * groups, LANES) for ref in (left, right)], axis=0)
     turned = scratch[...].T
     rows = swap_blocks([turned[k * C:(k + 1) * C, :] for k in range(LANES // C)], C)
     block[0, :LANES, :] = jnp.concatenate(rows, axis=0).astype(BF16)
@@ -159,13 +157,17 @@
     return [cot[half, pl.ds(pl.multiple_of((col * 2 + t) * per_row, per_row), per_row), :] for t in range(2)]
 
 
-def near_kernel(rows, near, weight, lefts, cot, grads, far_mix, spread_right, weight_dc):
+def near_kernel(rows, near, weight, sent, lefts, cot, grads, far_mix, spread_right, weight_dc):
     slots = near.shape[0]
     row, col = lax.axis_index("row"), lax.axis_index("col")
     tokens = 2 * slots
     spread(near, col, slots, 0, lefts, tokens)
     spread(near, col, slots, 2 * C, spread_right, tokens)
     spread_cot(near, col, slots, rows, cot)
+    span = tokens * C
+    sent[:span, :] = lefts[...].astype(BF16)
+    for slot in range(slots):
+        sent[pl.ds(pl.multiple_of(span + (col ^ slot) * 2 * C, 2 * C), 2 * C), :] = near[slot, 2 * C:4 * C, :]
     all_weight = weight[...]
     weight_dc[...] = jnp.swapaxes(all_weight.astype(F32).reshape(C, C, LANES), 0, 1).reshape(C * C, LANES).astype(BF16)
     mix = mixing_rows(weight_dc[...], left_cots(cot, row, col, slots))
@@ -215,10 +217,9 @@
 
 
 def outer_kernel(
-    rows, own_lefts, own_rights, other, cot_all, weight, bias, left_in, right_in,
+    rows, slots, own_lefts, own_rights, other, cot_all, weight, bias, left_in, right_in,
     pair_out, left_out, right_out, weight_out, spread_left, lefts, rights, pair_block, weight_grad, sems,
 ):
-    slots = other.shape[0] // rows
     row, col, rep = lax.axis_index("row"), lax.axis_index("col"), lax.axis_index("rep")
     copies = [
         pltpu.make_async_copy(left_in, left_out, sems.at[0]),
@@ -228,17 +229,22 @@
         copy.start()
     per_row, per_col = 2 * slots, 2 * rows
     tokens = rows * per_row
-    for half in range(rows):
-        first = lax.rem(row + half, rows) * per_row
-        for slot in range(slots):
-            for t in range(2):
-                at = first + (col ^ slot) * 2 + t
-                block = other[half * slots + slot, t * C:(t + 1) * C, :]
-                spread_left[pl.ds(at, C, stride=tokens), :] = block.astype(F32)
+    span = per_row * C
+    stride = (other.shape[0] - 2 * span) // slots
+    for slot in range(slots):
+        for t in range(2):
+            at = 2 * span + slot * stride + t * C
+            spread_left[pl.ds((col ^ slot) * 2 + t, C, stride=per_row), :] = other[at:at + C, :].astype(F32)
+    near = other[:span, :].astype(F32).reshape(C, per_row, LANES)
+    both = ordered(row == 0, near, spread_left[...].reshape(C, per_row, LANES))
     lefts[rep] = own_lefts[...]
-    lefts[1 - rep] = spread_left[...].astype(BF16)
+    lefts[1 - rep] = both.reshape(C * tokens, LANES).astype(BF16)
     rights[rep] = own_rights[...]
-    sort_rights(other.at[:slots], other.at[slots:], row, col, slots, rows, 2 * C, rights.at[1 - rep])
+    for q in range(slots):
+        at = pl.multiple_of((q * rows + row) * 2 * C, 2 * C)
+        rights[1 - rep, pl.ds(at, 2 * C), :] = other[span + q * 2 * C:span + (q + 1) * 2 * C, :]
+        at = pl.multiple_of(((col ^ q) * rows + 1 - row) * 2 * C, 2 * C)
+        rights[1 - rep, pl.ds(at, 2 * C), :] = other[2 * span + q * stride + 2 * C:2 * span + q * stride + 4 * C, :]
 
     def all_of(ref, at):
         return jnp.concatenate([ref[0, at, :], ref[1, at, :]], axis=1)
@@ -248,30 +254,15 @@
     groups = C // count
     means = [[[] for _ in range(groups)] for _ in range(count)]
     for g in range(groups):
-        left = all_of(lefts, slice(g * LANES, (g + 1) * LANES))
-        outer = lax.dot_general(right_all, left, NT, preferred_element_type=F32) * (1.0 / S)
+        if g % 2 == 0:
+            left = all_of(lefts, slice(g * LANES, (g + 2) * LANES))
+            wide = lax.dot_general(right_all, left, NT, preferred_element_type=F32) * (1.0 / S)
+        outer = wide[:, g % 2 * LANES:(g % 2 + 1) * LANES]
         for h in range(tokens // count):
             first = h * count * C
             blocks = [outer[first + k * C:first + (k + 1) * C, :] for k in range(count)]
             for c, mean in enumerate(skew_blocks(blocks, tokens)):
                 means[c][g].append(mean)
-    for c in range(count):
-        mean = jnp.concatenate([jnp.concatenate(halves, axis=1) for halves in means[c]], axis=0).astype(BF16)
-        cot = jnp.concatenate(
-            [
-                cot_all[at:at + tokens, :]
-                for h in range(tokens // count)
-                for at in [(h * count + (k - c) % count) * tokens for k in range(count)]
-            ],
-            axis=0,
-        )
-        part = jnp.dot(mean, cot, preferred_element_type=F32)
-        at = slice(c * C, (c + 1) * C)
-        weight_grad[:, at, :] = part.reshape(groups, C, LANES)
-        copy = pltpu.make_async_copy(weight_grad.at[:, at], weight_out.at[:, at], sems.at[3 + c])
-        copy.start()
-        copies.append(copy)
-
     own_count = per_col // 2
     at = pl.ds(pl.multiple_of((col * per_col + rep * own_count) * C, own_count * C), own_count * C)
     own = lax.dot_general(all_of(lefts, slice(None)), all_of(rights, at), NT, preferred_element_type=F32) * (1.0 / S)
@@ -289,6 +280,23 @@
     copy = pltpu.make_async_copy(pair_block, pair_out, sems.at[2])
     copy.start()
     copies.append(copy)
+    for c in range(count):
+        mean = jnp.concatenate([jnp.concatenate(halves, axis=1) for halves in means[c]], axis=0).astype(BF16)
+        cot = jnp.concatenate(
+            [
+                cot_all[at:at + tokens, :]
+                for h in range(tokens // count)
+                for at in [(h * count + (k - c) % count) * tokens for k in range(count)]
+            ],
+            axis=0,
+        )
+        part = jnp.dot(mean, cot, preferred_element_type=F32)
+        at = slice(c * C, (c + 1) * C)
+        weight_grad[:, at, :] = part.reshape(groups, C, LANES)
+        copy = pltpu.make_async_copy(weight_grad.at[:, at], weight_out.at[:, at], sems.at[3 + c])
+        copy.start()
+        copies.append(copy)
+
     for copy in copies:
         copy.wait()
 
@@ -328,25 +336,26 @@
         block = jnp.concatenate([block, arrived], axis=0)
         flip *= 2
     far = jnp.concatenate(far, axis=0)
-    other = exchange(jnp.concatenate([block, far], axis=0), "rep", 1, 2)
 
     lefts = array((half_span, seqs), F32)
     cots = array((rows, cols * held * per_row, e), F32)
-    near_lefts, near_cot, near_grads, far_mix = pl.pallas_call(
+    near_sent, near_lefts, near_cot, near_grads, far_mix = pl.pallas_call(
         functools.partial(near_kernel, rows),
         out_shape=(
+            array((2 * half_span, seqs), BF16),
             lefts,
             cots,
             array((2 * held * C, seqs), F32),
             array((held * C, half_span), BF16),
         ),
         in_specs=[vmem] * 2,
-        out_specs=(vmem,) * 4,
+        out_specs=(vmem,) * 5,
         scratch_shapes=[pltpu.VMEM((half_span, seqs), F32), pltpu.VMEM((C * C, e), BF16)],
         compiler_params=params,
         cost_estimate=pl.CostEstimate(flops=300_000_000, bytes_accessed=2_000_000, transcendentals=0),
         name="near_part",
     )(block, weight)
+    other = exchange(jnp.concatenate([near_sent, far.reshape(-1, seqs)], axis=0), "rep", 1, 2)
 
     own_lefts, own_rights, cot_all, left_grad, right_grad = pl.pallas_call(
         functools.partial(far_kernel, rows),
@@ -372,7 +381,7 @@
 
     split = (C * tokens // LANES, LANES // tokens * C, e)
     pair_out, left_grad, right_grad, weight_grad = pl.pallas_call(
-        functools.partial(outer_kernel, rows),
+        functools.partial(outer_kernel, rows, cols),
         out_shape=(
             array((per_row, per_col // 2, e), F32),
             array((held, width), BF16),
@@ -382,7 +391,7 @@
         in_specs=[vmem] * 8,
         out_specs=(anywhere,) * 4,
         scratch_shapes=[
-            pltpu.VMEM((tokens * C, seqs), F32),
+            pltpu.VMEM((half_span, seqs), F32),
             pltpu.VMEM((2, tokens * C, seqs), BF16),
             pltpu.VMEM((2, tokens * C, seqs), BF16),
             pltpu.VMEM((per_row, per_col // 2, e), F32),

time: 20.7 us -> 20.3 us (0.981)
  Pallas kernels: 4.98 us -> 4.7 us
    pallas_call x2, Pallas kernels: 3.12 us -> 2.83 us  [the longest x1 1.68 us: gather_plan(): pl.pallas_call(functools.partial(outer_kernel, rows, cols), out_shape=(ar...]
  transfers between devices with their start and end apart: 5 -> 5, of which waited for: 4 -> 4; matrix products, arithmetic and copies ran while one was open for 0% -> 0% of each run, Pallas kernels for 9% -> 10%
where the time goes in v4:
time: 20.3 us; the launch traced here: 20.2 us
  starting transfers between devices  9.57 us (47%)
  waiting for transfers between devices  5.09 us (25%)
  Pallas kernels  4.7 us (23%)
  between operations  0.71 us (3%)
    ppermute x5, starting transfers between devices, exchange(): return lax.ppermute(x, axis, [(k, k ^ flip) for k in range(size)])  9.57 us
    ppermute x5, waiting for transfers between devices, exchange(): return lax.ppermute(x, axis, [(k, k ^ flip) for k in range(size)])  5.09 us
    pallas_call x1, Pallas kernels, gather_plan(): pl.pallas_call(functools.partial(outer_kernel, rows, cols), out_shape=(ar...  1.68 us
    pallas_call x1, Pallas kernels, gather_plan(): pl.pallas_call(functools.partial(near_kernel, rows), out_shape=(array((2...  1.15 us
    pallas_call x1, Pallas kernels, gather_plan(): pl.pallas_call(block_kernel, out_shape=(array((1, 2 * held * C + per_row...  1.08 us
    pallas_call x1, Pallas kernels, gather_plan(): pl.pallas_call(functools.partial(far_kernel, rows), out_shape=(array((tok...  0.79 us
  transfers between devices with their start and end apart: 5, of which 4 were waited for; matrix products, arithmetic and copies ran while one was open for 0% of the time, Pallas kernels for 10%

profile of v4, /device:TPU:0, one launch (start us, length us, event | category | flops | bytes accessed | tf_op | source)
XLA Modules:
  0.0 20.2 jit_solution(14995354380178830547)
XLA Ops:
  0.6 0.0 copy-start
  0.6 1.1 %own_block.1 = (bf16[1,160,128]{2,1,0:T(8,128)(2,1)S(1)}, f32[1,128]{1,0:T(1,128)S(1)}) custom-call(bf16[2,4096]{1,0:T(2,128)(2,1)} %left_in.1, bf16[2,4096]{1,0:T(2,128)(2,1)} %right_in.1, bf16[8,4,128]{2,1,0:T(4,128)(2,1)} %cotangent_in.1, f32[1,128]{1,0:T(1,128)} %bitcast.4), custom_call_target="tpu_custom_call" | custom-call | tf_op jit(solution)/shard_map/own_block/pallas_call | solution.py:316
  1.7 3.1 %collective-permute-start = (bf16[1,160,128]{2,1,0:T(8,128)(2,1)S(1)}, bf16[1,160,128]{2,1,0:T(8,128)(2,1)S(1)}, u32[]{:S(2)}, u32[]{:S(2)}) collective-permute-start(bf16[1,160,128]{2,1,0:T(8,128)(2,1)S(1)} %get-tuple-element.20), channel_id=1, source_target_pairs={{0,2},{2,0},{4,6},{6,4},{1,3},{3,1},{5,7},{7,5},{8,10},{10,8},{12,... | collective-permute-start | bytes 122888 | tf_op jit(solution)/shard_map/ppermute | solution.py:52
  4.8 2.0 %collective-permute-done = bf16[1,160,128]{2,1,0:T(8,128)(2,1)S(1)} collective-permute-done((bf16[1,160,128]{2,1,0:T(8,128)(2,1)S(1)}, bf16[1,160,128]{2,1,0:T(8,128)(2,1)S(1)}, u32[]{:S(2)}, u32[]{:S(2)}) %collective-permute-start) | collective-permute-done | bytes 40992 | tf_op jit(solution)/shard_map/ppermute | solution.py:52
  6.8 3.1 %collective-permute-start.2 = (bf16[2,160,128]{2,1,0:T(8,128)(2,1)S(1)}, bf16[2,160,128]{2,1,0:T(8,128)(2,1)S(1)}, u32[]{:S(2)}, u32[]{:S(2)}) collective-permute-start(bf16[2,160,128]{2,1,0:T(8,128)(2,1)S(1)} %get-tuple-element.37), channel_id=1, source_target_pairs={{0,4},{2,6},{4,0},{6,2},{1,5},{3,7},{5,1},{7,3},{8,12},{10,14},{12... | collective-permute-start | bytes 245768 | tf_op jit(solution)/shard_map/ppermute | solution.py:52
  9.9 1.5 %collective-permute-start.1 = (bf16[2,160,128]{2,1,0:T(8,128)(2,1)S(1)}, bf16[2,160,128]{2,1,0:T(8,128)(2,1)S(1)}, u32[]{:S(2)}, u32[]{:S(2)}) collective-permute-start(bf16[2,160,128]{2,1,0:T(8,128)(2,1)S(1)} %get-tuple-element.37), channel_id=1, source_target_pairs={{0,8},{8,0},{1,9},{9,1},{2,10},{10,2},{3,11},{11,3},{4,12},{12,4},... | collective-permute-start | bytes 245768 | tf_op jit(solution)/shard_map/ppermute | solution.py:52
  11.4 0.9 %collective-permute-done.2 = bf16[2,160,128]{2,1,0:T(8,128)(2,1)S(1)} collective-permute-done((bf16[2,160,128]{2,1,0:T(8,128)(2,1)S(1)}, bf16[2,160,128]{2,1,0:T(8,128)(2,1)S(1)}, u32[]{:S(2)}, u32[]{:S(2)}) %collective-permute-start.2) | collective-permute-done | bytes 81952 | tf_op jit(solution)/shard_map/ppermute | solution.py:52
  12.3 1.8 %collective-permute-start.3 = (bf16[2,160,128]{2,1,0:T(8,128)(2,1)S(1)}, bf16[2,160,128]{2,1,0:T(8,128)(2,1)S(1)}, u32[]{:S(2)}, u32[]{:S(2)}) collective-permute-start(bf16[2,160,128]{2,1,0:T(8,128)(2,1)S(1)} %collective-permute-done.2), channel_id=1, source_target_pairs={{0,8},{8,0},{1,9},{9,1},{2,10},{10,2},{3,11},{11,3},{4,12},{12,4},... | collective-permute-start | bytes 245768 | tf_op jit(solution)/shard_map/ppermute | solution.py:52
  14.2 0.0 copy-done
  14.2 1.1 %near_part.1 = (bf16[512,128]{1,0:T(8,128)(2,1)S(1)}, f32[256,128]{1,0:T(8,128)S(1)}, f32[2,64,128]{2,1,0:T(8,128)S(1)}, f32[128,128]{1,0:T(8,128)S(1)}, bf16[64,256]{1,0:T(8,128)(2,1)S(1)}) custom-call(bf16[4,160,128]{2,1,0:T(8,128)(2,1)S(1)} %constant_dynamic-update-slice_fusion.4.near, bf16[1024,128]{1,0:T(8,128)(2,1)S(1)} %copy-done), custom_call_target="tpu_custom_call" | custom-call | flops 300000000 | bytes 2000000 | tf_op jit(solution)/shard_map/near_part/pallas_call | solution.py:342
  15.3 0.0 collective-permute-done.1
  15.4 1.4 %collective-permute-done.3 = bf16[2,160,128]{2,1,0:T(8,128)(2,1)S(1)} collective-permute-done((bf16[2,160,128]{2,1,0:T(8,128)(2,1)S(1)}, bf16[2,160,128]{2,1,0:T(8,128)(2,1)S(1)}, u32[]{:S(2)}, u32[]{:S(2)}) %collective-permute-start.3) | collective-permute-done | bytes 81952 | tf_op jit(solution)/shard_map/ppermute | solution.py:52
  16.8 0.1 collective-permute-start.4
  16.9 0.8 %far_part.1 = (bf16[512,128]{1,0:T(8,128)(2,1)S(1)}, bf16[512,128]{1,0:T(8,128)(2,1)S(1)}, bf16[256,128]{1,0:T(8,128)(2,1)S(1)}, bf16[2,4096]{1,0:T(2,128)(2,1)S(1)}, bf16[2,4096]{1,0:T(2,128)(2,1)S(1)}) custom-call(bf16[4,160,128]{2,1,0:T(8,128)(2,1)S(1)} %constant_dynamic-update-slice_fusion.2.far, ...), custom_call_target="tpu_custom_call" | custom-call | flops 10000000000 | bytes 1000000 | tf_op jit(solution)/shard_map/far_part/pallas_call | solution.py:360
  17.7 0.8 %collective-permute-done.4.other = bf16[1152,128]{1,0:T(8,128)(2,1)S(1)} collective-permute-done((bf16[1152,128]{1,0:T(8,128)(2,1)S(1)}, bf16[1152,128]{1,0:T(8,128)(2,1)S(1)}, u32[]{:S(2)}, u32[]{:S(2)}) %collective-permute-start.4) | collective-permute-done | bytes 294944 | tf_op jit(solution)/shard_map/ppermute | solution.py:52
  18.5 1.7 %outer_mean.1 = (f32[8,2,128]{2,1,0:T(2,128)}, bf16[2,4096]{1,0:T(2,128)(2,1)}, bf16[2,4096]{1,0:T(2,128)(2,1)}, f32[4,256,128]{2,1,0:T(8,128)}) custom-call(bf16[512,128]{1,0:T(8,128)(2,1)S(1)} %get-tuple-element.25.own_lefts, bf16[512,128]{1,0:T(8,128)(2,1)S(1)} %get-tuple-element.26.own_rights, bf16[1152,128]{1,0:T(8,128)(2,1)S(1)} %collective-permute-done.4.other, ...), custom_call_target="tpu_custom_call" | custom-call | tf_op jit(solution)/shard_map/outer_mean/pallas_call | solution.py:383
  (6 shorter events, 0.1 us)
Async XLA Ops:
  0.6 13.5 %copy-start = (bf16[1024,128]{1,0:T(8,128)(2,1)S(1)}, bf16[1024,128]{1,0:T(8,128)(2,1)}, u32[]{:S(2)}) copy-start(bf16[1024,128]{1,0:T(8,128)(2,1)} %weight.5) | copy-start | bytes 786436
  1.7 5.1 %collective-permute-start = (bf16[1,160,128]{2,1,0:T(8,128)(2,1)S(1)}, bf16[1,160,128]{2,1,0:T(8,128)(2,1)S(1)}, u32[]{:S(2)}, u32[]{:S(2)}) collective-permute-start(bf16[1,160,128]{2,1,0:T(8,128)(2,1)S(1)} %get-tuple-element.20), channel_id=1, source_target_pairs={{0,2},{2,0},{4,6},{6,4},{1,3},{3,1},{5,7},{7,5},{8,10},{10,8},{12,... | collective-permute-start | bytes 122888 | tf_op jit(solution)/shard_map/ppermute | solution.py:52
  6.8 5.5 %collective-permute-start.2 = (bf16[2,160,128]{2,1,0:T(8,128)(2,1)S(1)}, bf16[2,160,128]{2,1,0:T(8,128)(2,1)S(1)}, u32[]{:S(2)}, u32[]{:S(2)}) collective-permute-start(bf16[2,160,128]{2,1,0:T(8,128)(2,1)S(1)} %get-tuple-element.37), channel_id=1, source_target_pairs={{0,4},{2,6},{4,0},{6,2},{1,5},{3,7},{5,1},{7,3},{8,12},{10,14},{12... | collective-permute-start | bytes 245768 | tf_op jit(solution)/shard_map/ppermute | solution.py:52
  9.9 5.4 %collective-permute-start.1 = (bf16[2,160,128]{2,1,0:T(8,128)(2,1)S(1)}, bf16[2,160,128]{2,1,0:T(8,128)(2,1)S(1)}, u32[]{:S(2)}, u32[]{:S(2)}) collective-permute-start(bf16[2,160,128]{2,1,0:T(8,128)(2,1)S(1)} %get-tuple-element.37), channel_id=1, source_target_pairs={{0,8},{8,0},{1,9},{9,1},{2,10},{10,2},{3,11},{11,3},{4,12},{12,4},... | collective-permute-start | bytes 245768 | tf_op jit(solution)/shard_map/ppermute | solution.py:52
  12.3 4.4 %collective-permute-start.3 = (bf16[2,160,128]{2,1,0:T(8,128)(2,1)S(1)}, bf16[2,160,128]{2,1,0:T(8,128)(2,1)S(1)}, u32[]{:S(2)}, u32[]{:S(2)}) collective-permute-start(bf16[2,160,128]{2,1,0:T(8,128)(2,1)S(1)} %collective-permute-done.2), channel_id=1, source_target_pairs={{0,8},{8,0},{1,9},{9,1},{2,10},{10,2},{3,11},{11,3},{4,12},{12,4},... | collective-permute-start | bytes 245768 | tf_op jit(solution)/shard_map/ppermute | solution.py:52
  16.8 1.6 %collective-permute-start.4 = (bf16[1152,128]{1,0:T(8,128)(2,1)S(1)}, bf16[1152,128]{1,0:T(8,128)(2,1)S(1)}, u32[]{:S(2)}, u32[]{:S(2)}) collective-permute-start(bf16[1152,128]{1,0:T(8,128)(2,1)S(1)} %pad_maximum_fusion), channel_id=1, source_target_pairs={{0,1},{1,0},{2,3},{3,2},{4,5},{5,4},{6,7},{7,6},{8,9},{9,8},{10,11... | collective-permute-start | bytes 884744 | tf_op jit(solution)/shard_map/ppermute | solution.py:52

commit v5 on v4

--- a/solution.py
+++ b/solution.py
@@ -69,19 +69,24 @@
     return blocks
 
 
-def skew_blocks(blocks, width):
+def pick_diagonals(blocks, width, sign):
     count = len(blocks)
     lane_block = lax.broadcasted_iota(jnp.int32, blocks[0].shape, 1) // width
-    blocks = [pltpu.roll(x, k * width, 1) if k else x for k, x in enumerate(blocks)]
     bit = 1
     while bit < count:
         upper = (lane_block & bit) != 0
-        blocks = [jnp.where(upper, blocks[(m + bit) % count], blocks[m]) for m in range(count)]
+        blocks = [jnp.where(upper, blocks[(m + sign * bit) % count], blocks[m]) for m in range(count)]
         bit *= 2
+    return blocks
+
+
+def skew_blocks(blocks, width):
+    count = len(blocks)
+    blocks = pick_diagonals([pltpu.roll(x, k * width, 1) if k else x for k, x in enumerate(blocks)], width, 1)
     return [blocks[-c % count] for c in range(count)]
 
 
-def block_kernel(left_in, right_in, cotangent_in, bias_in, block, bias, left, right, cotangent, scratch, sems):
+def block_kernel(left_in, right_in, cotangent_in, bias_in, block, bias, left, right, cotangent, sems):
     pairs = ((left_in, left), (right_in, right), (cotangent_in, cotangent), (bias_in, bias))
     copies = [pltpu.make_async_copy(source, into, sems.at[k]) for k, (source, into) in enumerate(pairs)]
     for copy in copies:
@@ -90,9 +95,10 @@
         copy.wait()
     held, width = left.shape
     groups = width // LANES
-    scratch[...] = jnp.concatenate([ref[...].astype(F32).reshape(held * groups, LANES) for ref in (left, right)], axis=0)
-    turned = scratch[...].T
-    rows = swap_blocks([turned[k * C:(k + 1) * C, :] for k in range(LANES // C)], C)
+    parts = [ref[t:t + 1, :].astype(F32).reshape(groups, LANES) for ref in (left, right) for t in range(held)]
+    turned = jnp.concatenate(pick_diagonals(parts, C, -1), axis=0).T
+    parts = pick_diagonals([turned[k * C:(k + 1) * C, :] for k in range(LANES // C)], C, 1)
+    rows = [pltpu.roll(parts[-k], LANES - k * C, 1) if k else parts[0] for k in range(len(parts))]
     block[0, :LANES, :] = jnp.concatenate(rows, axis=0).astype(BF16)
     per_row, per_col, _ = cotangent.shape
     cot = cotangent[...].astype(F32)
@@ -217,7 +223,7 @@
 
 
 def outer_kernel(
-    rows, slots, own_lefts, own_rights, other, cot_all, weight, bias, left_in, right_in,
+    rows, slots, near_sent, own_lefts, own_rights, other, cot_all, weight, bias, left_in, right_in,
     pair_out, left_out, right_out, weight_out, spread_left, lefts, rights, pair_block, weight_grad, sems,
 ):
     row, col, rep = lax.axis_index("row"), lax.axis_index("col"), lax.axis_index("rep")
@@ -265,18 +271,19 @@
                 means[c][g].append(mean)
     own_count = per_col // 2
     at = pl.ds(pl.multiple_of((col * per_col + rep * own_count) * C, own_count * C), own_count * C)
-    own = lax.dot_general(all_of(lefts, slice(None)), all_of(rights, at), NT, preferred_element_type=F32) * (1.0 / S)
+    own_left = jnp.concatenate([near_sent[:span, :], other[:span, :]], axis=1)
+    own_right = jnp.concatenate([rights[rep, at, :], rights[1 - rep, at, :]], axis=1)
+    own = lax.dot_general(own_left, own_right, NT, preferred_element_type=F32) * (1.0 / S)
     own_mean = jnp.concatenate(
         [
-            jnp.concatenate([own[c * tokens:(c + 1) * tokens, t * C:(t + 1) * C] for c in range(C)], axis=1)
+            jnp.concatenate([own[c * per_row:(c + 1) * per_row, t * C:(t + 1) * C] for c in range(C)], axis=1)
             for t in range(own_count)
         ],
         axis=0,
     ).astype(BF16)
     own_pairs = jnp.dot(own_mean, weight[...], preferred_element_type=F32) + bias[...]
     for t in range(own_count):
-        lower = own_pairs[t * tokens:t * tokens + per_row, :]
-        pair_block[:, t, :] = jnp.where(row == 0, lower, own_pairs[t * tokens + per_row:(t + 1) * tokens, :])
+        pair_block[:, t, :] = own_pairs[t * per_row:(t + 1) * per_row, :]
     copy = pltpu.make_async_copy(pair_block, pair_out, sems.at[2])
     copy.start()
     copies.append(copy)
@@ -322,7 +329,6 @@
             pltpu.VMEM((held, width), BF16),
             pltpu.VMEM((held, width), BF16),
             pltpu.VMEM((per_row, per_col, e), BF16),
-            pltpu.VMEM((LANES, LANES), F32),
             pltpu.SemaphoreType.DMA((4,)),
         ],
         compiler_params=params,
@@ -388,7 +394,7 @@
             array((held, width), BF16),
             array(split, F32),
         ),
-        in_specs=[vmem] * 8,
+        in_specs=[vmem] * 9,
         out_specs=(anywhere,) * 4,
         scratch_shapes=[
             pltpu.VMEM((half_span, seqs), F32),
@@ -400,7 +406,7 @@
         ],
         compiler_params=params,
         name="outer_mean",
-    )(own_lefts, own_rights, other, cot_all, weight, bias_row, left_grad, right_grad)
+    )(near_sent, own_lefts, own_rights, other, cot_all, weight, bias_row, left_grad, right_grad)
     return pair_out, left_grad, right_grad, weight_grad.reshape(C * C, e)
 
 

time: 20.3 us -> 20.1 us (level)
  no operation moved by 1% of the time
where the time goes in v5:
time: 20.1 us; the launch traced here: 20 us
  starting transfers between devices  9.57 us (48%)
  waiting for transfers between devices  5.09 us (25%)
  Pallas kernels  4.52 us (22%)
  between operations  0.71 us (4%)
    ppermute x5, starting transfers between devices, exchange(): return lax.ppermute(x, axis, [(k, k ^ flip) for k in range(size)])  9.57 us
    ppermute x5, waiting for transfers between devices, exchange(): return lax.ppermute(x, axis, [(k, k ^ flip) for k in range(size)])  5.09 us
    pallas_call x1, Pallas kernels, gather_plan(): pl.pallas_call(functools.partial(outer_kernel, rows, cols), out_shape=(ar...  1.57 us
    pallas_call x1, Pallas kernels, gather_plan(): pl.pallas_call(functools.partial(near_kernel, rows), out_shape=(array((2...  1.15 us
    pallas_call x1, Pallas kernels, gather_plan(): pl.pallas_call(block_kernel, out_shape=(array((1, 2 * held * C + per_row...  1.01 us
    pallas_call x1, Pallas kernels, gather_plan(): pl.pallas_call(functools.partial(far_kernel, rows), out_shape=(array((tok...  0.79 us
  transfers between devices with their start and end apart: 5, of which 4 were waited for; matrix products, arithmetic and copies ran while one was open for 0% of the time, Pallas kernels for 10%

profile of v5, /device:TPU:0, one launch (start us, length us, event | category | flops | bytes accessed | tf_op | source)
XLA Modules:
  0.0 20.0 jit_solution(12270790829597121421)
XLA Ops:
  0.6 0.0 copy-start
  0.6 1.0 %own_block.1 = (bf16[1,160,128]{2,1,0:T(8,128)(2,1)S(1)}, f32[1,128]{1,0:T(1,128)S(1)}) custom-call(bf16[2,4096]{1,0:T(2,128)(2,1)} %left_in.1, bf16[2,4096]{1,0:T(2,128)(2,1)} %right_in.1, bf16[8,4,128]{2,1,0:T(4,128)(2,1)} %cotangent_in.1, f32[1,128]{1,0:T(1,128)} %bitcast.4), custom_call_target="tpu_custom_call" | custom-call | tf_op jit(solution)/shard_map/own_block/pallas_call | solution.py:323
  1.7 3.1 %collective-permute-start = (bf16[1,160,128]{2,1,0:T(8,128)(2,1)S(1)}, bf16[1,160,128]{2,1,0:T(8,128)(2,1)S(1)}, u32[]{:S(2)}, u32[]{:S(2)}) collective-permute-start(bf16[1,160,128]{2,1,0:T(8,128)(2,1)S(1)} %get-tuple-element.20), channel_id=1, source_target_pairs={{0,2},{2,0},{4,6},{6,4},{1,3},{3,1},{5,7},{7,5},{8,10},{10,8},{12,... | collective-permute-start | bytes 122888 | tf_op jit(solution)/shard_map/ppermute | solution.py:52
  4.8 2.0 %collective-permute-done = bf16[1,160,128]{2,1,0:T(8,128)(2,1)S(1)} collective-permute-done((bf16[1,160,128]{2,1,0:T(8,128)(2,1)S(1)}, bf16[1,160,128]{2,1,0:T(8,128)(2,1)S(1)}, u32[]{:S(2)}, u32[]{:S(2)}) %collective-permute-start) | collective-permute-done | bytes 40992 | tf_op jit(solution)/shard_map/ppermute | solution.py:52
  6.7 3.1 %collective-permute-start.1 = (bf16[2,160,128]{2,1,0:T(8,128)(2,1)S(1)}, bf16[2,160,128]{2,1,0:T(8,128)(2,1)S(1)}, u32[]{:S(2)}, u32[]{:S(2)}) collective-permute-start(bf16[2,160,128]{2,1,0:T(8,128)(2,1)S(1)} %get-tuple-element.36), channel_id=1, source_target_pairs={{0,4},{2,6},{4,0},{6,2},{1,5},{3,7},{5,1},{7,3},{8,12},{10,14},{12... | collective-permute-start | bytes 245768 | tf_op jit(solution)/shard_map/ppermute | solution.py:52
  9.8 1.5 %collective-permute-start.2 = (bf16[2,160,128]{2,1,0:T(8,128)(2,1)S(1)}, bf16[2,160,128]{2,1,0:T(8,128)(2,1)S(1)}, u32[]{:S(2)}, u32[]{:S(2)}) collective-permute-start(bf16[2,160,128]{2,1,0:T(8,128)(2,1)S(1)} %get-tuple-element.36), channel_id=1, source_target_pairs={{0,8},{8,0},{1,9},{9,1},{2,10},{10,2},{3,11},{11,3},{4,12},{12,4},... | collective-permute-start | bytes 245768 | tf_op jit(solution)/shard_map/ppermute | solution.py:52
  11.3 0.9 %collective-permute-done.1 = bf16[2,160,128]{2,1,0:T(8,128)(2,1)S(1)} collective-permute-done((bf16[2,160,128]{2,1,0:T(8,128)(2,1)S(1)}, bf16[2,160,128]{2,1,0:T(8,128)(2,1)S(1)}, u32[]{:S(2)}, u32[]{:S(2)}) %collective-permute-start.1) | collective-permute-done | bytes 81952 | tf_op jit(solution)/shard_map/ppermute | solution.py:52
  12.3 1.8 %collective-permute-start.3 = (bf16[2,160,128]{2,1,0:T(8,128)(2,1)S(1)}, bf16[2,160,128]{2,1,0:T(8,128)(2,1)S(1)}, u32[]{:S(2)}, u32[]{:S(2)}) collective-permute-start(bf16[2,160,128]{2,1,0:T(8,128)(2,1)S(1)} %collective-permute-done.1), channel_id=1, source_target_pairs={{0,8},{8,0},{1,9},{9,1},{2,10},{10,2},{3,11},{11,3},{4,12},{12,4},... | collective-permute-start | bytes 245768 | tf_op jit(solution)/shard_map/ppermute | solution.py:52
  14.1 0.0 copy-done
  14.1 1.1 %near_part.1 = (bf16[512,128]{1,0:T(8,128)(2,1)S(1)}, f32[256,128]{1,0:T(8,128)S(1)}, f32[2,64,128]{2,1,0:T(8,128)S(1)}, f32[128,128]{1,0:T(8,128)S(1)}, bf16[64,256]{1,0:T(8,128)(2,1)S(1)}) custom-call(bf16[4,160,128]{2,1,0:T(8,128)(2,1)S(1)} %constant_dynamic-update-slice_fusion.2.near, bf16[1024,128]{1,0:T(8,128)(2,1)S(1)} %copy-done), custom_call_target="tpu_custom_call" | custom-call | flops 300000000 | bytes 2000000 | tf_op jit(solution)/shard_map/near_part/pallas_call | solution.py:348
  15.3 0.0 collective-permute-done.2
  15.3 1.4 %collective-permute-done.3 = bf16[2,160,128]{2,1,0:T(8,128)(2,1)S(1)} collective-permute-done((bf16[2,160,128]{2,1,0:T(8,128)(2,1)S(1)}, bf16[2,160,128]{2,1,0:T(8,128)(2,1)S(1)}, u32[]{:S(2)}, u32[]{:S(2)}) %collective-permute-start.3) | collective-permute-done | bytes 81952 | tf_op jit(solution)/shard_map/ppermute | solution.py:52
  16.8 0.1 collective-permute-start.4
  16.8 0.8 %far_part.1 = (bf16[512,128]{1,0:T(8,128)(2,1)S(1)}, bf16[512,128]{1,0:T(8,128)(2,1)S(1)}, bf16[256,128]{1,0:T(8,128)(2,1)S(1)}, bf16[2,4096]{1,0:T(2,128)(2,1)S(1)}, bf16[2,4096]{1,0:T(2,128)(2,1)S(1)}) custom-call(bf16[4,160,128]{2,1,0:T(8,128)(2,1)S(1)} %constant_dynamic-update-slice_fusion.5.far, ...), custom_call_target="tpu_custom_call" | custom-call | flops 10000000000 | bytes 1000000 | tf_op jit(solution)/shard_map/far_part/pallas_call | solution.py:366
  17.6 0.8 %collective-permute-done.4.other = bf16[1152,128]{1,0:T(8,128)(2,1)S(1)} collective-permute-done((bf16[1152,128]{1,0:T(8,128)(2,1)S(1)}, bf16[1152,128]{1,0:T(8,128)(2,1)S(1)}, u32[]{:S(2)}, u32[]{:S(2)}) %collective-permute-start.4) | collective-permute-done | bytes 294944 | tf_op jit(solution)/shard_map/ppermute | solution.py:52
  18.4 1.6 %outer_mean.1 = (f32[8,2,128]{2,1,0:T(2,128)}, bf16[2,4096]{1,0:T(2,128)(2,1)}, bf16[2,4096]{1,0:T(2,128)(2,1)}, f32[4,256,128]{2,1,0:T(8,128)}) custom-call(bf16[512,128]{1,0:T(8,128)(2,1)S(1)} %get-tuple-element.21.near_sent, bf16[512,128]{1,0:T(8,128)(2,1)S(1)} %get-tuple-element.26.own_lefts, bf16[512,128]{1,0:T(8,128)(2,1)S(1)} %get-tuple-element.27.own_rights, ...), custom_call_target="tpu_custom_call" | custom-call | tf_op jit(solution)/shard_map/outer_mean/pallas_call | solution.py:389
  (6 shorter events, 0.1 us)
Async XLA Ops:
  0.6 13.5 %copy-start = (bf16[1024,128]{1,0:T(8,128)(2,1)S(1)}, bf16[1024,128]{1,0:T(8,128)(2,1)}, u32[]{:S(2)}) copy-start(bf16[1024,128]{1,0:T(8,128)(2,1)} %weight.5) | copy-start | bytes 786436
  1.7 5.1 %collective-permute-start = (bf16[1,160,128]{2,1,0:T(8,128)(2,1)S(1)}, bf16[1,160,128]{2,1,0:T(8,128)(2,1)S(1)}, u32[]{:S(2)}, u32[]{:S(2)}) collective-permute-start(bf16[1,160,128]{2,1,0:T(8,128)(2,1)S(1)} %get-tuple-element.20), channel_id=1, source_target_pairs={{0,2},{2,0},{4,6},{6,4},{1,3},{3,1},{5,7},{7,5},{8,10},{10,8},{12,... | collective-permute-start | bytes 122888 | tf_op jit(solution)/shard_map/ppermute | solution.py:52
  6.7 5.5 %collective-permute-start.1 = (bf16[2,160,128]{2,1,0:T(8,128)(2,1)S(1)}, bf16[2,160,128]{2,1,0:T(8,128)(2,1)S(1)}, u32[]{:S(2)}, u32[]{:S(2)}) collective-permute-start(bf16[2,160,128]{2,1,0:T(8,128)(2,1)S(1)} %get-tuple-element.36), channel_id=1, source_target_pairs={{0,4},{2,6},{4,0},{6,2},{1,5},{3,7},{5,1},{7,3},{8,12},{10,14},{12... | collective-permute-start | bytes 245768 | tf_op jit(solution)/shard_map/ppermute | solution.py:52
  9.8 5.4 %collective-permute-start.2 = (bf16[2,160,128]{2,1,0:T(8,128)(2,1)S(1)}, bf16[2,160,128]{2,1,0:T(8,128)(2,1)S(1)}, u32[]{:S(2)}, u32[]{:S(2)}) collective-permute-start(bf16[2,160,128]{2,1,0:T(8,128)(2,1)S(1)} %get-tuple-element.36), channel_id=1, source_target_pairs={{0,8},{8,0},{1,9},{9,1},{2,10},{10,2},{3,11},{11,3},{4,12},{12,4},... | collective-permute-start | bytes 245768 | tf_op jit(solution)/shard_map/ppermute | solution.py:52
  12.3 4.4 %collective-permute-start.3 = (bf16[2,160,128]{2,1,0:T(8,128)(2,1)S(1)}, bf16[2,160,128]{2,1,0:T(8,128)(2,1)S(1)}, u32[]{:S(2)}, u32[]{:S(2)}) collective-permute-start(bf16[2,160,128]{2,1,0:T(8,128)(2,1)S(1)} %collective-permute-done.1), channel_id=1, source_target_pairs={{0,8},{8,0},{1,9},{9,1},{2,10},{10,2},{3,11},{11,3},{4,12},{12,4},... | collective-permute-start | bytes 245768 | tf_op jit(solution)/shard_map/ppermute | solution.py:52
  16.8 1.6 %collective-permute-start.4 = (bf16[1152,128]{1,0:T(8,128)(2,1)S(1)}, bf16[1152,128]{1,0:T(8,128)(2,1)S(1)}, u32[]{:S(2)}, u32[]{:S(2)}) collective-permute-start(bf16[1152,128]{1,0:T(8,128)(2,1)S(1)} %pad_maximum_fusion), channel_id=1, source_target_pairs={{0,1},{1,0},{2,3},{3,2},{4,5},{5,4},{6,7},{7,6},{8,9},{9,8},{10,11... | collective-permute-start | bytes 884744 | tf_op jit(solution)/shard_map/ppermute | solution.py:52

commit v6 on v5

--- a/solution.py
+++ b/solution.py
@@ -361,7 +361,7 @@
         cost_estimate=pl.CostEstimate(flops=300_000_000, bytes_accessed=2_000_000, transcendentals=0),
         name="near_part",
     )(block, weight)
-    other = exchange(jnp.concatenate([near_sent, far.reshape(-1, seqs)], axis=0), "rep", 1, 2)
+    other = exchange(jnp.concatenate([near_sent, far[:, :2 * held * C].reshape(-1, seqs)], axis=0), "rep", 1, 2)
 
     own_lefts, own_rights, cot_all, left_grad, right_grad = pl.pallas_call(
         functools.partial(far_kernel, rows),

time: 20.1 us -> 20.1 us (level)
  no operation moved by 1% of the time
where the time goes in v6:
time: 20.1 us; the launch traced here: 19.9 us
  starting transfers between devices  9.57 us (48%)
  waiting for transfers between devices  5.04 us (25%)
  Pallas kernels  4.52 us (22%)
  between operations  0.72 us (4%)
    ppermute x5, starting transfers between devices, exchange(): return lax.ppermute(x, axis, [(k, k ^ flip) for k in range(size)])  9.57 us
    ppermute x5, waiting for transfers between devices, exchange(): return lax.ppermute(x, axis, [(k, k ^ flip) for k in range(size)])  5.04 us
    pallas_call x1, Pallas kernels, gather_plan(): pl.pallas_call(functools.partial(outer_kernel, rows, cols), out_shape=(ar...  1.57 us
    pallas_call x1, Pallas kernels, gather_plan(): pl.pallas_call(functools.partial(near_kernel, rows), out_shape=(array((2...  1.15 us
    pallas_call x1, Pallas kernels, gather_plan(): pl.pallas_call(block_kernel, out_shape=(array((1, 2 * held * C + per_row...  1.01 us
    pallas_call x1, Pallas kernels, gather_plan(): pl.pallas_call(functools.partial(far_kernel, rows), out_shape=(array((tok...  0.79 us
  transfers between devices with their start and end apart: 5, of which 4 were waited for; matrix products, arithmetic and copies ran while one was open for 0% of the time, Pallas kernels for 10%

profile of v6, /device:TPU:0, one launch (start us, length us, event | category | flops | bytes accessed | tf_op | source)
XLA Modules:
  0.0 19.9 jit_solution(12295016188332541466)
XLA Ops:
  0.6 0.0 copy-start
  0.6 1.0 %own_block.1 = (bf16[1,160,128]{2,1,0:T(8,128)(2,1)S(1)}, f32[1,128]{1,0:T(1,128)S(1)}) custom-call(bf16[2,4096]{1,0:T(2,128)(2,1)} %left_in.1, bf16[2,4096]{1,0:T(2,128)(2,1)} %right_in.1, bf16[8,4,128]{2,1,0:T(4,128)(2,1)} %cotangent_in.1, f32[1,128]{1,0:T(1,128)} %bitcast.4), custom_call_target="tpu_custom_call" | custom-call | tf_op jit(solution)/shard_map/own_block/pallas_call | solution.py:323
  1.7 3.1 %collective-permute-start = (bf16[1,160,128]{2,1,0:T(8,128)(2,1)S(1)}, bf16[1,160,128]{2,1,0:T(8,128)(2,1)S(1)}, u32[]{:S(2)}, u32[]{:S(2)}) collective-permute-start(bf16[1,160,128]{2,1,0:T(8,128)(2,1)S(1)} %get-tuple-element.20), channel_id=1, source_target_pairs={{0,2},{2,0},{4,6},{6,4},{1,3},{3,1},{5,7},{7,5},{8,10},{10,8},{12,... | collective-permute-start | bytes 122888 | tf_op jit(solution)/shard_map/ppermute | solution.py:52
  4.8 2.0 %collective-permute-done = bf16[1,160,128]{2,1,0:T(8,128)(2,1)S(1)} collective-permute-done((bf16[1,160,128]{2,1,0:T(8,128)(2,1)S(1)}, bf16[1,160,128]{2,1,0:T(8,128)(2,1)S(1)}, u32[]{:S(2)}, u32[]{:S(2)}) %collective-permute-start) | collective-permute-done | bytes 40992 | tf_op jit(solution)/shard_map/ppermute | solution.py:52
  6.7 3.1 %collective-permute-start.1 = (bf16[2,160,128]{2,1,0:T(8,128)(2,1)S(1)}, bf16[2,160,128]{2,1,0:T(8,128)(2,1)S(1)}, u32[]{:S(2)}, u32[]{:S(2)}) collective-permute-start(bf16[2,160,128]{2,1,0:T(8,128)(2,1)S(1)} %get-tuple-element.36), channel_id=1, source_target_pairs={{0,4},{2,6},{4,0},{6,2},{1,5},{3,7},{5,1},{7,3},{8,12},{10,14},{12... | collective-permute-start | bytes 245768 | tf_op jit(solution)/shard_map/ppermute | solution.py:52
  9.8 1.5 %collective-permute-start.2 = (bf16[2,160,128]{2,1,0:T(8,128)(2,1)S(1)}, bf16[2,160,128]{2,1,0:T(8,128)(2,1)S(1)}, u32[]{:S(2)}, u32[]{:S(2)}) collective-permute-start(bf16[2,160,128]{2,1,0:T(8,128)(2,1)S(1)} %get-tuple-element.36), channel_id=1, source_target_pairs={{0,8},{8,0},{1,9},{9,1},{2,10},{10,2},{3,11},{11,3},{4,12},{12,4},... | collective-permute-start | bytes 245768 | tf_op jit(solution)/shard_map/ppermute | solution.py:52
  11.3 0.9 %collective-permute-done.1 = bf16[2,160,128]{2,1,0:T(8,128)(2,1)S(1)} collective-permute-done((bf16[2,160,128]{2,1,0:T(8,128)(2,1)S(1)}, bf16[2,160,128]{2,1,0:T(8,128)(2,1)S(1)}, u32[]{:S(2)}, u32[]{:S(2)}) %collective-permute-start.1) | collective-permute-done | bytes 81952 | tf_op jit(solution)/shard_map/ppermute | solution.py:52
  12.3 1.8 %collective-permute-start.3 = (bf16[2,160,128]{2,1,0:T(8,128)(2,1)S(1)}, bf16[2,160,128]{2,1,0:T(8,128)(2,1)S(1)}, u32[]{:S(2)}, u32[]{:S(2)}) collective-permute-start(bf16[2,160,128]{2,1,0:T(8,128)(2,1)S(1)} %collective-permute-done.1), channel_id=1, source_target_pairs={{0,8},{8,0},{1,9},{9,1},{2,10},{10,2},{3,11},{11,3},{4,12},{12,4},... | collective-permute-start | bytes 245768 | tf_op jit(solution)/shard_map/ppermute | solution.py:52
  14.1 0.0 copy-done
  14.1 1.1 %near_part.1 = (bf16[512,128]{1,0:T(8,128)(2,1)S(1)}, f32[256,128]{1,0:T(8,128)S(1)}, f32[2,64,128]{2,1,0:T(8,128)S(1)}, f32[128,128]{1,0:T(8,128)S(1)}, bf16[64,256]{1,0:T(8,128)(2,1)S(1)}) custom-call(bf16[4,160,128]{2,1,0:T(8,128)(2,1)S(1)} %constant_dynamic-update-slice_fusion.2.near, bf16[1024,128]{1,0:T(8,128)(2,1)S(1)} %copy-done), custom_call_target="tpu_custom_call" | custom-call | flops 300000000 | bytes 2000000 | tf_op jit(solution)/shard_map/near_part/pallas_call | solution.py:348
  15.3 0.0 collective-permute-done.2
  15.3 1.4 %collective-permute-done.3 = bf16[2,160,128]{2,1,0:T(8,128)(2,1)S(1)} collective-permute-done((bf16[2,160,128]{2,1,0:T(8,128)(2,1)S(1)}, bf16[2,160,128]{2,1,0:T(8,128)(2,1)S(1)}, u32[]{:S(2)}, u32[]{:S(2)}) %collective-permute-start.3) | collective-permute-done | bytes 81952 | tf_op jit(solution)/shard_map/ppermute | solution.py:52
  16.8 0.1 collective-permute-start.4
  16.8 0.8 %far_part.1 = (bf16[512,128]{1,0:T(8,128)(2,1)S(1)}, bf16[512,128]{1,0:T(8,128)(2,1)S(1)}, bf16[256,128]{1,0:T(8,128)(2,1)S(1)}, bf16[2,4096]{1,0:T(2,128)(2,1)S(1)}, bf16[2,4096]{1,0:T(2,128)(2,1)S(1)}) custom-call(bf16[4,160,128]{2,1,0:T(8,128)(2,1)S(1)} %constant_dynamic-update-slice_fusion.5.far, ...), custom_call_target="tpu_custom_call" | custom-call | flops 10000000000 | bytes 1000000 | tf_op jit(solution)/shard_map/far_part/pallas_call | solution.py:366
  17.6 0.7 %collective-permute-done.4.other = bf16[1024,128]{1,0:T(8,128)(2,1)S(1)} collective-permute-done((bf16[1024,128]{1,0:T(8,128)(2,1)S(1)}, bf16[1024,128]{1,0:T(8,128)(2,1)S(1)}, u32[]{:S(2)}, u32[]{:S(2)}) %collective-permute-start.4) | collective-permute-done | bytes 262176 | tf_op jit(solution)/shard_map/ppermute | solution.py:52
  18.4 1.6 %outer_mean.1 = (f32[8,2,128]{2,1,0:T(2,128)}, bf16[2,4096]{1,0:T(2,128)(2,1)}, bf16[2,4096]{1,0:T(2,128)(2,1)}, f32[4,256,128]{2,1,0:T(8,128)}) custom-call(bf16[512,128]{1,0:T(8,128)(2,1)S(1)} %get-tuple-element.21.near_sent, bf16[512,128]{1,0:T(8,128)(2,1)S(1)} %get-tuple-element.26.own_lefts, bf16[512,128]{1,0:T(8,128)(2,1)S(1)} %get-tuple-element.27.own_rights, ...), custom_call_target="tpu_custom_call" | custom-call | tf_op jit(solution)/shard_map/outer_mean/pallas_call | solution.py:389
  (7 shorter events, 0.1 us)
Async XLA Ops:
  0.6 13.5 %copy-start = (bf16[1024,128]{1,0:T(8,128)(2,1)S(1)}, bf16[1024,128]{1,0:T(8,128)(2,1)}, u32[]{:S(2)}) copy-start(bf16[1024,128]{1,0:T(8,128)(2,1)} %weight.5) | copy-start | bytes 786436
  1.7 5.1 %collective-permute-start = (bf16[1,160,128]{2,1,0:T(8,128)(2,1)S(1)}, bf16[1,160,128]{2,1,0:T(8,128)(2,1)S(1)}, u32[]{:S(2)}, u32[]{:S(2)}) collective-permute-start(bf16[1,160,128]{2,1,0:T(8,128)(2,1)S(1)} %get-tuple-element.20), channel_id=1, source_target_pairs={{0,2},{2,0},{4,6},{6,4},{1,3},{3,1},{5,7},{7,5},{8,10},{10,8},{12,... | collective-permute-start | bytes 122888 | tf_op jit(solution)/shard_map/ppermute | solution.py:52
  6.7 5.5 %collective-permute-start.1 = (bf16[2,160,128]{2,1,0:T(8,128)(2,1)S(1)}, bf16[2,160,128]{2,1,0:T(8,128)(2,1)S(1)}, u32[]{:S(2)}, u32[]{:S(2)}) collective-permute-start(bf16[2,160,128]{2,1,0:T(8,128)(2,1)S(1)} %get-tuple-element.36), channel_id=1, source_target_pairs={{0,4},{2,6},{4,0},{6,2},{1,5},{3,7},{5,1},{7,3},{8,12},{10,14},{12... | collective-permute-start | bytes 245768 | tf_op jit(solution)/shard_map/ppermute | solution.py:52
  9.8 5.4 %collective-permute-start.2 = (bf16[2,160,128]{2,1,0:T(8,128)(2,1)S(1)}, bf16[2,160,128]{2,1,0:T(8,128)(2,1)S(1)}, u32[]{:S(2)}, u32[]{:S(2)}) collective-permute-start(bf16[2,160,128]{2,1,0:T(8,128)(2,1)S(1)} %get-tuple-element.36), channel_id=1, source_target_pairs={{0,8},{8,0},{1,9},{9,1},{2,10},{10,2},{3,11},{11,3},{4,12},{12,4},... | collective-permute-start | bytes 245768 | tf_op jit(solution)/shard_map/ppermute | solution.py:52
  12.3 4.4 %collective-permute-start.3 = (bf16[2,160,128]{2,1,0:T(8,128)(2,1)S(1)}, bf16[2,160,128]{2,1,0:T(8,128)(2,1)S(1)}, u32[]{:S(2)}, u32[]{:S(2)}) collective-permute-start(bf16[2,160,128]{2,1,0:T(8,128)(2,1)S(1)} %collective-permute-done.1), channel_id=1, source_target_pairs={{0,8},{8,0},{1,9},{9,1},{2,10},{10,2},{3,11},{11,3},{4,12},{12,4},... | collective-permute-start | bytes 245768 | tf_op jit(solution)/shard_map/ppermute | solution.py:52
  16.8 1.6 %collective-permute-start.4 = (bf16[1024,128]{1,0:T(8,128)(2,1)S(1)}, bf16[1024,128]{1,0:T(8,128)(2,1)S(1)}, u32[]{:S(2)}, u32[]{:S(2)}) collective-permute-start(bf16[1024,128]{1,0:T(8,128)(2,1)S(1)} %pad_maximum_fusion), channel_id=1, source_target_pairs={{0,1},{1,0},{2,3},{3,2},{4,5},{5,4},{6,7},{7,6},{8,9},{9,8},{10,11... | collective-permute-start | bytes 786440 | tf_op jit(solution)/shard_map/ppermute | solution.py:52

commit v7 on v6

--- a/solution.py
+++ b/solution.py
@@ -262,7 +262,7 @@
     for g in range(groups):
         if g % 2 == 0:
             left = all_of(lefts, slice(g * LANES, (g + 2) * LANES))
-            wide = lax.dot_general(right_all, left, NT, preferred_element_type=F32) * (1.0 / S)
+            wide = lax.dot_general(right_all, left, NT, preferred_element_type=F32)
         outer = wide[:, g % 2 * LANES:(g % 2 + 1) * LANES]
         for h in range(tokens // count):
             first = h * count * C
@@ -297,7 +297,7 @@
             ],
             axis=0,
         )
-        part = jnp.dot(mean, cot, preferred_element_type=F32)
+        part = jnp.dot(mean, cot, preferred_element_type=F32) * (1.0 / S)
         at = slice(c * C, (c + 1) * C)
         weight_grad[:, at, :] = part.reshape(groups, C, LANES)
         copy = pltpu.make_async_copy(weight_grad.at[:, at], weight_out.at[:, at], sems.at[3 + c])

time: 20.1 us -> 20.1 us (level)
  no operation moved by 1% of the time
where the time goes in v7:
time: 20.1 us; the launch traced here: 20 us
  starting transfers between devices  9.57 us (48%)
  waiting for transfers between devices  5.04 us (25%)
  Pallas kernels  4.53 us (23%)
  between operations  0.72 us (4%)
    ppermute x5, starting transfers between devices, exchange(): return lax.ppermute(x, axis, [(k, k ^ flip) for k in range(size)])  9.57 us
    ppermute x5, waiting for transfers between devices, exchange(): return lax.ppermute(x, axis, [(k, k ^ flip) for k in range(size)])  5.04 us
    pallas_call x1, Pallas kernels, gather_plan(): pl.pallas_call(functools.partial(outer_kernel, rows, cols), out_shape=(ar...  1.58 us
    pallas_call x1, Pallas kernels, gather_plan(): pl.pallas_call(functools.partial(near_kernel, rows), out_shape=(array((2...  1.15 us
    pallas_call x1, Pallas kernels, gather_plan(): pl.pallas_call(block_kernel, out_shape=(array((1, 2 * held * C + per_row...  1.01 us
    pallas_call x1, Pallas kernels, gather_plan(): pl.pallas_call(functools.partial(far_kernel, rows), out_shape=(array((tok...  0.79 us
  transfers between devices with their start and end apart: 5, of which 4 were waited for; matrix products, arithmetic and copies ran while one was open for 0% of the time, Pallas kernels for 10%

profile of v7, /device:TPU:0, one launch (start us, length us, event | category | flops | bytes accessed | tf_op | source)
XLA Modules:
  0.0 20.0 jit_solution(1198316272674300847)
XLA Ops:
  0.6 0.0 copy-start
  0.6 1.0 %own_block.1 = (bf16[1,160,128]{2,1,0:T(8,128)(2,1)S(1)}, f32[1,128]{1,0:T(1,128)S(1)}) custom-call(bf16[2,4096]{1,0:T(2,128)(2,1)} %left_in.1, bf16[2,4096]{1,0:T(2,128)(2,1)} %right_in.1, bf16[8,4,128]{2,1,0:T(4,128)(2,1)} %cotangent_in.1, f32[1,128]{1,0:T(1,128)} %bitcast.4), custom_call_target="tpu_custom_call" | custom-call | tf_op jit(solution)/shard_map/own_block/pallas_call | solution.py:323
  1.7 3.1 %collective-permute-start = (bf16[1,160,128]{2,1,0:T(8,128)(2,1)S(1)}, bf16[1,160,128]{2,1,0:T(8,128)(2,1)S(1)}, u32[]{:S(2)}, u32[]{:S(2)}) collective-permute-start(bf16[1,160,128]{2,1,0:T(8,128)(2,1)S(1)} %get-tuple-element.20), channel_id=1, source_target_pairs={{0,2},{2,0},{4,6},{6,4},{1,3},{3,1},{5,7},{7,5},{8,10},{10,8},{12,... | collective-permute-start | bytes 122888 | tf_op jit(solution)/shard_map/ppermute | solution.py:52
  4.8 2.0 %collective-permute-done = bf16[1,160,128]{2,1,0:T(8,128)(2,1)S(1)} collective-permute-done((bf16[1,160,128]{2,1,0:T(8,128)(2,1)S(1)}, bf16[1,160,128]{2,1,0:T(8,128)(2,1)S(1)}, u32[]{:S(2)}, u32[]{:S(2)}) %collective-permute-start) | collective-permute-done | bytes 40992 | tf_op jit(solution)/shard_map/ppermute | solution.py:52
  6.7 3.1 %collective-permute-start.1 = (bf16[2,160,128]{2,1,0:T(8,128)(2,1)S(1)}, bf16[2,160,128]{2,1,0:T(8,128)(2,1)S(1)}, u32[]{:S(2)}, u32[]{:S(2)}) collective-permute-start(bf16[2,160,128]{2,1,0:T(8,128)(2,1)S(1)} %get-tuple-element.36), channel_id=1, source_target_pairs={{0,4},{2,6},{4,0},{6,2},{1,5},{3,7},{5,1},{7,3},{8,12},{10,14},{12... | collective-permute-start | bytes 245768 | tf_op jit(solution)/shard_map/ppermute | solution.py:52
  9.8 1.5 %collective-permute-start.2 = (bf16[2,160,128]{2,1,0:T(8,128)(2,1)S(1)}, bf16[2,160,128]{2,1,0:T(8,128)(2,1)S(1)}, u32[]{:S(2)}, u32[]{:S(2)}) collective-permute-start(bf16[2,160,128]{2,1,0:T(8,128)(2,1)S(1)} %get-tuple-element.36), channel_id=1, source_target_pairs={{0,8},{8,0},{1,9},{9,1},{2,10},{10,2},{3,11},{11,3},{4,12},{12,4},... | collective-permute-start | bytes 245768 | tf_op jit(solution)/shard_map/ppermute | solution.py:52
  11.3 0.9 %collective-permute-done.1 = bf16[2,160,128]{2,1,0:T(8,128)(2,1)S(1)} collective-permute-done((bf16[2,160,128]{2,1,0:T(8,128)(2,1)S(1)}, bf16[2,160,128]{2,1,0:T(8,128)(2,1)S(1)}, u32[]{:S(2)}, u32[]{:S(2)}) %collective-permute-start.1) | collective-permute-done | bytes 81952 | tf_op jit(solution)/shard_map/ppermute | solution.py:52
  12.3 1.8 %collective-permute-start.3 = (bf16[2,160,128]{2,1,0:T(8,128)(2,1)S(1)}, bf16[2,160,128]{2,1,0:T(8,128)(2,1)S(1)}, u32[]{:S(2)}, u32[]{:S(2)}) collective-permute-start(bf16[2,160,128]{2,1,0:T(8,128)(2,1)S(1)} %collective-permute-done.1), channel_id=1, source_target_pairs={{0,8},{8,0},{1,9},{9,1},{2,10},{10,2},{3,11},{11,3},{4,12},{12,4},... | collective-permute-start | bytes 245768 | tf_op jit(solution)/shard_map/ppermute | solution.py:52
  14.1 0.0 copy-done
  14.1 1.1 %near_part.1 = (bf16[512,128]{1,0:T(8,128)(2,1)S(1)}, f32[256,128]{1,0:T(8,128)S(1)}, f32[2,64,128]{2,1,0:T(8,128)S(1)}, f32[128,128]{1,0:T(8,128)S(1)}, bf16[64,256]{1,0:T(8,128)(2,1)S(1)}) custom-call(bf16[4,160,128]{2,1,0:T(8,128)(2,1)S(1)} %constant_dynamic-update-slice_fusion.2.near, bf16[1024,128]{1,0:T(8,128)(2,1)S(1)} %copy-done), custom_call_target="tpu_custom_call" | custom-call | flops 300000000 | bytes 2000000 | tf_op jit(solution)/shard_map/near_part/pallas_call | solution.py:348
  15.3 0.0 collective-permute-done.2
  15.3 1.4 %collective-permute-done.3 = bf16[2,160,128]{2,1,0:T(8,128)(2,1)S(1)} collective-permute-done((bf16[2,160,128]{2,1,0:T(8,128)(2,1)S(1)}, bf16[2,160,128]{2,1,0:T(8,128)(2,1)S(1)}, u32[]{:S(2)}, u32[]{:S(2)}) %collective-permute-start.3) | collective-permute-done | bytes 81952 | tf_op jit(solution)/shard_map/ppermute | solution.py:52
  16.8 0.1 collective-permute-start.4
  16.8 0.8 %far_part.1 = (bf16[512,128]{1,0:T(8,128)(2,1)S(1)}, bf16[512,128]{1,0:T(8,128)(2,1)S(1)}, bf16[256,128]{1,0:T(8,128)(2,1)S(1)}, bf16[2,4096]{1,0:T(2,128)(2,1)S(1)}, bf16[2,4096]{1,0:T(2,128)(2,1)S(1)}) custom-call(bf16[4,160,128]{2,1,0:T(8,128)(2,1)S(1)} %constant_dynamic-update-slice_fusion.5.far, ...), custom_call_target="tpu_custom_call" | custom-call | flops 10000000000 | bytes 1000000 | tf_op jit(solution)/shard_map/far_part/pallas_call | solution.py:366
  17.6 0.7 %collective-permute-done.4.other = bf16[1024,128]{1,0:T(8,128)(2,1)S(1)} collective-permute-done((bf16[1024,128]{1,0:T(8,128)(2,1)S(1)}, bf16[1024,128]{1,0:T(8,128)(2,1)S(1)}, u32[]{:S(2)}, u32[]{:S(2)}) %collective-permute-start.4) | collective-permute-done | bytes 262176 | tf_op jit(solution)/shard_map/ppermute | solution.py:52
  18.4 1.6 %outer_mean.1 = (f32[8,2,128]{2,1,0:T(2,128)}, bf16[2,4096]{1,0:T(2,128)(2,1)}, bf16[2,4096]{1,0:T(2,128)(2,1)}, f32[4,256,128]{2,1,0:T(8,128)}) custom-call(bf16[512,128]{1,0:T(8,128)(2,1)S(1)} %get-tuple-element.21.near_sent, bf16[512,128]{1,0:T(8,128)(2,1)S(1)} %get-tuple-element.26.own_lefts, bf16[512,128]{1,0:T(8,128)(2,1)S(1)} %get-tuple-element.27.own_rights, ...), custom_call_target="tpu_custom_call" | custom-call | tf_op jit(solution)/shard_map/outer_mean/pallas_call | solution.py:389
  (7 shorter events, 0.1 us)
Async XLA Ops:
  0.6 13.5 %copy-start = (bf16[1024,128]{1,0:T(8,128)(2,1)S(1)}, bf16[1024,128]{1,0:T(8,128)(2,1)}, u32[]{:S(2)}) copy-start(bf16[1024,128]{1,0:T(8,128)(2,1)} %weight.5) | copy-start | bytes 786436
  1.7 5.1 %collective-permute-start = (bf16[1,160,128]{2,1,0:T(8,128)(2,1)S(1)}, bf16[1,160,128]{2,1,0:T(8,128)(2,1)S(1)}, u32[]{:S(2)}, u32[]{:S(2)}) collective-permute-start(bf16[1,160,128]{2,1,0:T(8,128)(2,1)S(1)} %get-tuple-element.20), channel_id=1, source_target_pairs={{0,2},{2,0},{4,6},{6,4},{1,3},{3,1},{5,7},{7,5},{8,10},{10,8},{12,... | collective-permute-start | bytes 122888 | tf_op jit(solution)/shard_map/ppermute | solution.py:52
  6.7 5.5 %collective-permute-start.1 = (bf16[2,160,128]{2,1,0:T(8,128)(2,1)S(1)}, bf16[2,160,128]{2,1,0:T(8,128)(2,1)S(1)}, u32[]{:S(2)}, u32[]{:S(2)}) collective-permute-start(bf16[2,160,128]{2,1,0:T(8,128)(2,1)S(1)} %get-tuple-element.36), channel_id=1, source_target_pairs={{0,4},{2,6},{4,0},{6,2},{1,5},{3,7},{5,1},{7,3},{8,12},{10,14},{12... | collective-permute-start | bytes 245768 | tf_op jit(solution)/shard_map/ppermute | solution.py:52
  9.8 5.4 %collective-permute-start.2 = (bf16[2,160,128]{2,1,0:T(8,128)(2,1)S(1)}, bf16[2,160,128]{2,1,0:T(8,128)(2,1)S(1)}, u32[]{:S(2)}, u32[]{:S(2)}) collective-permute-start(bf16[2,160,128]{2,1,0:T(8,128)(2,1)S(1)} %get-tuple-element.36), channel_id=1, source_target_pairs={{0,8},{8,0},{1,9},{9,1},{2,10},{10,2},{3,11},{11,3},{4,12},{12,4},... | collective-permute-start | bytes 245768 | tf_op jit(solution)/shard_map/ppermute | solution.py:52
  12.3 4.4 %collective-permute-start.3 = (bf16[2,160,128]{2,1,0:T(8,128)(2,1)S(1)}, bf16[2,160,128]{2,1,0:T(8,128)(2,1)S(1)}, u32[]{:S(2)}, u32[]{:S(2)}) collective-permute-start(bf16[2,160,128]{2,1,0:T(8,128)(2,1)S(1)} %collective-permute-done.1), channel_id=1, source_target_pairs={{0,8},{8,0},{1,9},{9,1},{2,10},{10,2},{3,11},{11,3},{4,12},{12,4},... | collective-permute-start | bytes 245768 | tf_op jit(solution)/shard_map/ppermute | solution.py:52
  16.8 1.6 %collective-permute-start.4 = (bf16[1024,128]{1,0:T(8,128)(2,1)S(1)}, bf16[1024,128]{1,0:T(8,128)(2,1)S(1)}, u32[]{:S(2)}, u32[]{:S(2)}) collective-permute-start(bf16[1024,128]{1,0:T(8,128)(2,1)S(1)} %pad_maximum_fusion), channel_id=1, source_target_pairs={{0,1},{1,0},{2,3},{3,2},{4,5},{5,4},{6,7},{7,6},{8,9},{9,8},{10,11... | collective-permute-start | bytes 786440 | tf_op jit(solution)/shard_map/ppermute | solution.py:52
